TPU v7x, 128 devices: a whole 4x4x4 slice. The times are simulated.
128 devices in a mesh: lat: 8 (over y, x_lo), lon: 16 (over z, x_hi, core).
Axes of the slice: x: 4 (x_hi: 2, x_lo: 2; x = x_hi * 2 + x_lo), y: 4, z: 4, core: 2. Of those that a mesh axis runs over, the one named last changes fastest.
Arguments:
- control: float32 [120, 512, 4320], P(None, 'lat', 'lon'), may hold values from -6 to 6
- land_mask: int32 [30, 512, 4320], P(None, 'lat', 'lon'), may hold values 0 or 1
- row_class: int32 [512], P('lat'), may hold values from 0 to 15
- decay_rate: float32 [16], replicated, may hold values from 0.004 to 0.05, as said below
- balance: float32 [120, 120], replicated, may hold values from -0.2 to 1.2
Outputs:
- increment: float32 [120, 512, 4320], P(None, 'lat', 'lon')
- velocity: float32 [2, 30, 512, 4320], P(None, None, 'lat', 'lon')
Inputs may be any that keep to these rules, and one draw needn't show every extreme that they name: `decay_rate`: a third or more of the entries are 0.02 or more.
All inputs are finite; a program needn't handle non-finite values. No bound on the sum of `land_mask` on one device may be relied on, other than what follows from the above.
Results may differ from a plain program's by a relative error of at most 0.00019.
Values sent between devices are 32-bit elements; how exact they have to be, the bound alone decides.
A program may use at most 192 MiB of HBM per device.

v0:
```python
import math

import jax
import jax.numpy as jnp
from jax import lax
from jax.sharding import PartitionSpec as P

LON_DEV = 270


def carried_in(value, axis, join, neutral, backward):
    count, mine = (lax.axis_size(axis), lax.axis_index(axis))
    pieces = jax.tree.map(lambda part: lax.all_gather(part, axis), value)
    if backward:
        pieces = jax.tree.map(lambda part: part[::-1], pieces)
        mine = count - 1 - mine
    running = jax.tree.map(
        lambda part, zero: jnp.full_like(part, 0) + jnp.asarray(zero, part.dtype), value, neutral
    )

    def step(position, running):
        longer = join(running, jax.tree.map(lambda part: part[position], pieces))
        return jax.tree.map(lambda new, old: jnp.where(position < mine, new, old), longer, running)

    return lax.fori_loop(0, count - 1, step, running)


def extended(block, sides, width, periodic):
    for axis, dim in sides:
        count = lax.axis_size(axis)
        forward = [(i, i + 1) for i in range(count - 1)]
        if periodic:
            forward.append((count - 1, 0))
        backward = [(target, source) for source, target in forward]
        low = lax.ppermute(
            lax.slice_in_dim(block, block.shape[dim] - width, None, axis=dim), axis, forward
        )
        high = lax.ppermute(lax.slice_in_dim(block, 0, width, axis=dim), axis, backward)
        block = jnp.concatenate([low, block, high], axis=dim)
    return block


def link(earlier, later):
    return (earlier[0] * later[0], later[0] * earlier[1] + later[1])


def sector_sweep(field_values, retention_factor, scale_factor, forward_sweep, carry_signal):
    components, band_rows, extent = field_values.shape
    sector = LON_DEV
    blocks_total = extent // sector
    offsets = jnp.arange(sector, dtype=jnp.float32)
    offset_grid = offsets[:, None] - offsets[None, :]
    if not forward_sweep:
        offset_grid = -offset_grid
    powered = jnp.power(retention_factor[:, None, None], jnp.maximum(offset_grid, 0.0)[None])
    kernel = jnp.where(offset_grid[None] >= 0.0, powered, 0.0) * scale_factor[:, None, None]
    tiles = field_values.reshape(components, band_rows, blocks_total, sector)
    local = jnp.einsum("rjk,crbk->crbj", kernel, tiles, precision=lax.Precision.HIGHEST)
    if forward_sweep:
        trailing_values = local[..., -1]
        profile = jnp.power(retention_factor[:, None], offsets[None, :] + 1.0)
    else:
        trailing_values = local[..., 0]
        profile = jnp.power(retention_factor[:, None], sector - offsets[None, :])
    block_damping = jnp.power(retention_factor, jnp.float32(sector))
    inbound_state = carry_signal(trailing_values, block_damping, forward_sweep)
    result = local + inbound_state[..., None] * profile[None, :, None, :]
    return result.reshape(components, band_rows, extent)


def block_carries(trailing_values, block_damping, forward_sweep):
    series = jnp.moveaxis(trailing_values, 2, 0)

    def advance(carried, value):
        return (block_damping[None, :] * carried + value, carried)

    closing, before = lax.scan(
        advance, jnp.zeros(series.shape[1:], jnp.float32), series, reverse=not forward_sweep
    )
    blocks_total = series.shape[0]
    block_index = jnp.arange(blocks_total, dtype=jnp.float32)
    if forward_sweep:
        lifted = jnp.power(block_damping[:, None], block_index[None, :])
    else:
        lifted = jnp.power(block_damping[:, None], blocks_total - 1.0 - block_index[None, :])
    wrapped = closing / (1.0 - jnp.power(block_damping, jnp.float32(blocks_total)))[None, :]
    return jnp.moveaxis(before, 0, 2) + lifted[None] * wrapped[:, :, None]


def band_pass(field_values, retention_factor, scale_factor, forward_sweep):
    band_rows = field_values.shape[1]
    log_keep = jnp.log(retention_factor)
    running = jnp.cumsum(log_keep)
    row_index = jnp.arange(band_rows)
    if forward_sweep:
        exponent = running[:, None] - running[None, :]
        allowed = row_index[:, None] >= row_index[None, :]
        profile = jnp.exp(running)
    else:
        shifted = running - log_keep
        exponent = shifted[None, :] - shifted[:, None]
        allowed = row_index[None, :] >= row_index[:, None]
        profile = jnp.exp(running[-1] - shifted)
    kernel = jnp.where(allowed, jnp.exp(jnp.minimum(exponent, 0.0)), 0.0) * scale_factor[None, :]
    local = jnp.einsum("ik,ckj->cij", kernel, field_values, precision=lax.Precision.HIGHEST)
    band_decay = jnp.exp(running[-1]).reshape(1, 1)
    neutral = (jnp.ones_like(band_decay), jnp.zeros((local.shape[0], local.shape[2]), jnp.float32))
    if forward_sweep:
        closing, before = carried_in((band_decay, local[:, -1, :]), "lat", link, neutral, False)
    else:
        closing, before = carried_in((band_decay, local[:, 0, :]), "lat", link, neutral, True)
    return local + profile[None, :, None] * before[:, None, :]


def body(control, land_mask, row_class, decay_rate, balance):
    components, band_rows, sector = control.shape
    levels = land_mask.shape[0]
    groups = components // levels
    classes = decay_rate.shape[0]
    one_hot = (row_class[:, None] == jnp.arange(classes, dtype=jnp.int32)[None, :]).astype(
        jnp.float32
    )
    decay = jnp.sum(one_hot * decay_rate[None, :], axis=1)
    retention_factor = 1.0 - decay
    forward_gain = jnp.sqrt(decay * (2.0 - decay))
    weights = land_mask.astype(jnp.float32)

    def masked(field_values):
        return (field_values.reshape(groups, levels, band_rows, sector) * weights[None]).reshape(
            components, band_rows, sector
        )

    masked_in = masked(control)
    piece = lax.all_to_all(masked_in, "lon", split_axis=1, concat_axis=2, tiled=True)
    share_rows = piece.shape[1]
    first_row = lax.axis_index("lon") * share_rows
    retain_part = lax.dynamic_slice_in_dim(retention_factor, first_row, share_rows)
    gain_part = lax.dynamic_slice_in_dim(forward_gain, first_row, share_rows)
    decay_part = lax.dynamic_slice_in_dim(decay, first_row, share_rows)
    eastward = sector_sweep(piece, retain_part, gain_part, True, block_carries)
    westward = sector_sweep(eastward, retain_part, decay_part, False, block_carries)
    smooth = lax.all_to_all(westward, "lon", split_axis=2, concat_axis=1, tiled=True)
    northward = band_pass(smooth, retention_factor, decay, True)
    southward = band_pass(northward, retention_factor, decay, False)
    filtered = masked(southward)
    mixed = jnp.einsum("ck,krj->crj", balance, filtered, precision=lax.Precision.HIGHEST)
    increment = masked(mixed)
    pressure = increment.reshape(groups, levels, band_rows, sector)[groups - 1]
    rows_halo = extended(pressure, (("lat", 1),), 1, False)
    cols_halo = extended(pressure, (("lon", 2),), 1, True)
    merid_diff = (rows_halo[:, 2:, :] - rows_halo[:, :-2, :]) * 0.5
    zonal_diff = (cols_halo[:, :, 2:] - cols_halo[:, :, :-2]) * 0.5
    global_row = lax.axis_index("lat").astype(jnp.float32) * band_rows + jnp.arange(
        band_rows, dtype=jnp.float32
    )
    latitude = (-70.0 + 140.0 * (global_row + 0.5) / (band_rows * lax.axis_size("lat"))) * (
        math.pi / 180.0
    )
    sine_lat = jnp.sin(latitude)
    coriolis_inverse = sine_lat / (sine_lat * sine_lat + 0.01)
    east_speed = -coriolis_inverse[None, :, None] * merid_diff * weights
    north_speed = coriolis_inverse[None, :, None] * zonal_diff * weights
    velocity = jnp.stack([east_speed, north_speed])
    return (increment, velocity)


def solution(mesh):
    return jax.shard_map(
        body,
        mesh=mesh,
        in_specs=(P(None, "lat", "lon"), P(None, "lat", "lon"), P("lat"), P(), P()),
        out_specs=(P(None, "lat", "lon"), P(None, None, "lat", "lon")),
        check_vma=False,
    )
```

profile of v0, /device:TPU:0, one launch (start us, length us, event | category | flops | bytes accessed | tf_op | source)
XLA Modules:
  0.0 672.6 jit_solution(5995320904670312220)
XLA Ops:
  0.6 2.1 convert_element_type.7
  2.7 5.8 mul.283
  8.5 11.4 %copy.131 = f32[120,64,270]{0,1,2:T(8,128)} copy(f32[120,64,270]{2,1,0:T(8,128)} %bitcast.108) | data formatting | bytes 16588800 | tf_op jit(solution)/shard_map/mul | solution.py:129
  19.9 12.6 %mul.285 = f32[120,64,270]{0,1,2:T(8,128)} multiply(f32[120,64,270]{0,1,2:T(8,128)} %param.13, f32[120,64,270]{0,1,2:T(8,128)} %copy.131) | non-fusion elementwise | flops 2073600 | bytes 24883200 | tf_op jit(solution)/shard_map/mul | solution.py:129
  32.6 12.0 %copy.132 = f32[120,64,270]{0,2,1:T(8,128)} copy(f32[120,64,270]{0,1,2:T(8,128)} %mul.285) | data formatting | bytes 16588800 | tf_op jit(solution)/shard_map/mul | solution.py:129
  44.6 8.1 %all-to-all-start = ((f32[120,64,270]{0,2,1:T(8,128)}), f32[120,64,270]{0,2,1:T(8,128)}, u32[]{:S(2)}, u32[]{:S(2)}) async-start(f32[120,64,270]{0,2,1:T(8,128)} %copy.132), calls=%async_computation | async-start | bytes 17825792 | tf_op jit(solution)/shard_map/all_to_all | solution.py:134
  59.9 95.3 %all-to-all-done = f32[120,64,270]{0,2,1:T(8,128)} async-done(((f32[120,64,270]{0,2,1:T(8,128)}), f32[120,64,270]{0,2,1:T(8,128)}, u32[]{:S(2)}, u32[]{:S(2)}) %all-to-all-start) | async-done | bytes 8294432 | tf_op jit(solution)/shard_map/all_to_all | solution.py:134
  155.1 11.4 %copy.133 = f32[120,16,4,270]{3,1,0,2:T(8,128)} copy(f32[120,16,4,270]{0,3,2,1:T(8,128)} %bitcast.1) | data formatting | bytes 16588800 | tf_op jit(solution)/shard_map/all_to_all | solution.py:134
  166.6 29.6 %fusion.19 = f32[120,4,16,270]{3,2,0,1:T(8,128)S(1)} fusion(f32[120,16,4,270]{3,1,0,2:T(8,128)} %copy.133, f32[4]{0:T(128)} %dynamic_slice.51, f32[270,270]{1,0:T(8,128)S(1)} %fusion.56, f32[4]{0:T(128)} %copy-done.9, pred[270,270]{1,0:T(8,128)(4,1)S(1)} %fusion.57), kind=kOutput, calls=%fused_computation.32 | convolution fusion | flops 6719047168 | bytes 16953332 | tf_op jit(solution)/shard_map/rjk,crbk->crbj/dot_general | solution.py:58
  196.2 4.3 copy-done.2
  200.4 3.0 slice.63
  203.4 3.6 copy.134
  207.6 22.1 %while.58 = (s32[]{:T(128)}, f32[120,4]{0,1:T(4,128)S(1)}, f32[16,120,4]{1,2,0:T(4,128)}, f32[4]{0:T(128)S(1)}, f32[16,120,4]{1,0,2:T(8,128)}, /*index=5*/s32[]{:T(128)}, s32[]{:T(128)}) while((s32[]{:T(128)}, f32[120,4]{0,1:T(4,128)S(1)}, f32[16,120,4]{1,2,0:T(4,128)}, f32[4]{0:T(128)S(1)}, f32[16,120,4]{1,0,2:T(8,128)}, ...), condition=%wide.region_2.3_spmd.clone, body=%wide.region_1.2_spmd.clone.sunk | while | flops 1923 | bytes 13688 | solution.py:77
  233.4 29.9 %fusion.16 = f32[120,4,16,270]{3,2,0,1:T(8,128)S(1)} fusion(f32[120,4,16,270]{3,2,0,1:T(8,128)} %copy-done.2, f32[4,270]{1,0:T(4,128)S(1)} %get-tuple-element.566, f32[120,4,16]{2,0,1:T(8,128)} %copy.136, f32[4]{0:T(128)} %dynamic_slice.52, f32[270,270]{1,0:T(8,128)S(1)} %copy-done.7, f32[4]{0:T(128)} %copy-done.9, pred[270,270]{1,0:T(8,128)(4,1)S(1)} %copy-done.8), kind=kOutput, calls=%fused_computation.31 | convolution fusion | flops 6723194368 | bytes 16988372 | tf_op jit(solution)/shard_map/rjk,crbk->crbj/dot_general | solution.py:58
  263.4 4.3 copy-done.1
  267.7 2.2 slice.64
  269.8 3.0 copy.137
  274.7 10.1 %multiply_add_fusion.2 = f32[120,4,16,270]{3,2,0,1:T(8,128)} fusion(f32[120,4,16,270]{3,2,0,1:T(8,128)} %copy-done.1, f32[4,270]{1,0:T(4,128)S(1)} %copy-done.11, f32[120,4,16]{2,0,1:T(8,128)S(1)} %copy.139), kind=kLoop, calls=%fused_computation.15 | loop fusion | flops 4147200 | bytes 16623840 | tf_op jit(solution)/shard_map/add | solution.py:67
  284.9 10.3 %copy.168 = f32[120,4,16,270]{0,1,3,2:T(4,128)} copy(f32[120,4,16,270]{3,2,0,1:T(8,128)} %multiply_add_fusion.2) | data formatting | bytes 16588800 | tf_op jit(solution)/shard_map/reshape | solution.py:68
  295.1 4.9 all-to-all-start.1
  302.2 108.9 %all-reduce = f32[8]{0:T(128)S(1)} all-reduce(f32[8]{0:T(128)S(1)} %dynamic-update-slice), channel_id=1, replica_groups=mesh['lat'=8,'lon'=16] {'lat'}, use_global_device_ids=true, to_apply=%add | all-reduce | flops 8 | bytes 64
  411.0 11.3 %copy.155 = f32[120,64,270]{0,2,1:T(8,128)} copy(f32[120,64,270]{2,1,0:T(8,128)} %bitcast.109) | data formatting | bytes 16588800 | tf_op jit(solution)/shard_map/mul | solution.py:129
  422.5 7.7 %copy.180 = f32[120,4,16,270]{0,3,2,1:T(8,128)} copy(f32[120,4,16,270]{0,1,3,2:T(4,128)} %bitcast.15) | data formatting | bytes 16588800 | tf_op jit(solution)/shard_map/all_to_all | solution.py:142
  430.2 12.6 %copy.143 = f32[120,16,4,270]{0,2,1,3:T(4,128)} copy(f32[120,16,4,270]{0,3,1,2:T(8,128)} %bitcast.110) | data formatting | bytes 16588800 | tf_op jit(solution)/shard_map/all_to_all | solution.py:142
  442.9 10.8 %convolution_bitcast_fusion = f32[120,64,270]{0,1,2:T(8,128)S(1)} fusion(f32[120,64,270]{0,1,2:T(8,128)} %bitcast.112, f32[64]{0:T(128)S(1)} %copy-done.15, f32[64]{0:T(128)S(1)} %copy-done.13), kind=kOutput, calls=%fused_computation.34 | convolution fusion | flops 1592545280 | bytes 16589312 | tf_op jit(solution)/shard_map/ik,ckj->cij/dot_general | solution.py:105
  453.7 3.4 copy-done.4
  458.1 34.2 %all-gather = f32[960,1,270]{2,1,0:T(1,128)S(1)} all-gather(f32[120,1,270]{2,1,0:T(1,128)} %copy.145), channel_id=2, replica_groups=mesh['lat'=8,'lon'=16] {'lat'}, dimensions={0}, use_global_device_ids=true | all-gather | bytes 1166400 | tf_op jit(solution)/shard_map/all_gather | solution.py:13
  493.5 16.5 %while.60 = (s32[]{:T(128)}, f32[120,270]{1,0:T(8,128)S(1)}, s32[]{:T(128)}, f32[8,1,1]{0,2,1:T(1,128)S(1)}, f32[8,120,270]{2,1,0:T(8,128)}, /*index=5*/s32[]{:T(128)}, s32[]{:T(128)}) while((s32[]{:T(128)}, f32[120,270]{1,0:T(8,128)S(1)}, s32[]{:T(128)}, f32[8,1,1]{0,2,1:T(1,128)S(1)}, f32[8,120,270]{2,1,0:T(8,128)}, ...), condition=%wide.region_7.8_spmd.clone, body=%wide.region_6.7_spmd.clone.sunk | while | flops 129604 | bytes 388925 | solution.py:25
  494.3 1.7 fusion.92
  496.7 1.7 fusion.92
  499.0 1.7 fusion.92
  501.3 1.7 fusion.92
  510.2 12.0 %fusion.25 = f32[120,64,270]{0,1,2:T(8,128)S(1)} fusion(f32[120,64,270]{0,1,2:T(8,128)} %copy-done.4, f32[120,270]{0,1:T(8,128)S(1)} %copy.148, f32[64]{0:T(128)S(1)} %copy-done.19, f32[64]{0:T(128)S(1)} %copy-done.16, f32[64]{0:T(128)S(1)} %copy-done.15), kind=kOutput, calls=%fused_computation.35 | convolution fusion | flops 1596692480 | bytes 16719168 | tf_op jit(solution)/shard_map/ik,ckj->cij/dot_general | solution.py:105
  522.2 3.4 copy-done.3
  526.0 36.0 %all-gather.1 = f32[960,1,270]{2,1,0:T(1,128)} all-gather(f32[120,1,270]{2,1,0:T(1,128)S(1)} %copy.149), channel_id=3, replica_groups=mesh['lat'=8,'lon'=16] {'lat'}, dimensions={0}, use_global_device_ids=true | all-gather | bytes 1166400 | tf_op jit(solution)/shard_map/all_gather | solution.py:13
  562.0 4.7 copy.150
  566.7 2.8 reshape.260
  569.5 2.6 rev.7
  572.1 20.4 %while.61 = (s32[]{:T(128)}, f32[120,270]{1,0:T(8,128)S(1)}, s32[]{:T(128)}, f32[8,1,1]{0,2,1:T(1,128)S(1)}, f32[8,120,270]{1,0,2:T(8,128)}, /*index=5*/s32[]{:T(128)}, s32[]{:T(128)}) while((s32[]{:T(128)}, f32[120,270]{1,0:T(8,128)S(1)}, s32[]{:T(128)}, f32[8,1,1]{0,2,1:T(1,128)S(1)}, f32[8,120,270]{1,0,2:T(8,128)}, ...), condition=%wide.region_9.10_spmd.clone, body=%wide.region_8.9_spmd.clone.sunk | while | flops 129604 | bytes 907325 | solution.py:25
  592.6 13.0 %add_multiply_fusion = f32[120,64,270]{0,1,2:T(8,128)} fusion(f32[120,64,270]{0,1,2:T(8,128)} %copy.131, f32[120,64,270]{0,1,2:T(8,128)} %copy-done.3, f32[120,270]{0,1:T(8,128)S(1)} %copy.152, f32[64]{0:T(128)S(1)} %copy-done.18), kind=kLoop, calls=%fused_computation.22 | loop fusion | flops 6220800 | bytes 25013056 | tf_op jit(solution)/shard_map/mul | solution.py:129
  605.6 21.2 %fusion.88 = (f32[120,64,270]{0,2,1:T(8,128)}, f32[120,64,270]{0,2,1:T(8,128)}) fusion(f32[120,64,270]{0,2,1:T(8,128)} %copy.155, f32[120,120]{1,0:T(8,128)S(1)} %copy-done, f32[120,64,270]{0,1,2:T(8,128)} %add_multiply_fusion), kind=kOutput, calls=%fused_computation.127 | convolution fusion | flops 2988057600 | bytes 33235200 | tf_op jit(solution)/shard_map/ck,krj->crj/dot_general | solution.py:146
  626.8 11.4 %copy.156 = f32[120,64,270]{2,1,0:T(8,128)} copy(f32[120,64,270]{0,2,1:T(8,128)} %get-tuple-element.568) | data formatting | bytes 16588800 | tf_op jit(solution)/shard_map/ck,krj->crj/dot_general | solution.py:146
  638.2 2.4 fusion.36
  642.6 1.7 collective-permute-start.1
  646.5 5.4 collective-permute-start.2
  652.0 10.1 %copy.161 = f32[120,64,270]{0,1,2:T(8,128)} copy(f32[120,64,270]{0,2,1:T(8,128)} %get-tuple-element.567) | data formatting | bytes 16588800
  664.8 4.6 fusion.35
  669.4 3.0 pad_maximum_fusion
  (233 shorter events, 78.0 us)
Async XLA Ops:
  0.6 604.9 %copy-start = (f32[120,120]{1,0:T(8,128)S(1)}, f32[120,120]{1,0:T(8,128)}, u32[]{:S(2)}) copy-start(f32[120,120]{1,0:T(8,128)} %param.17) | copy-start | bytes 172804
  44.5 8.2 %copy-start.20 = (f32[16]{0:T(128)S(1)}, f32[16]{0:T(128)}, u32[]{:S(2)}) copy-start(f32[16]{0:T(128)} %param.16) | copy-start | bytes 196
  44.6 8.2 %copy-start.21 = (s32[64]{0:T(128)S(1)}, s32[64]{0:T(128)}, u32[]{:S(2)}) copy-start(s32[64]{0:T(128)} %param.15) | copy-start | bytes 772
  44.6 110.6 %all-to-all-start = ((f32[120,64,270]{0,2,1:T(8,128)}), f32[120,64,270]{0,2,1:T(8,128)}, u32[]{:S(2)}, u32[]{:S(2)}) async-start(f32[120,64,270]{0,2,1:T(8,128)} %copy.132), calls=%async_computation | async-start | bytes 17825792 | tf_op jit(solution)/shard_map/all_to_all | solution.py:134
  52.8 4.0 copy-start.14
  53.7 3.1 copy-start.12
  56.7 1.8 copy-start.9
  196.2 4.3 copy-start.2
  200.4 33.0 %copy-start.7 = (f32[270,270]{1,0:T(8,128)S(1)}, f32[270,270]{1,0:T(8,128)}, u32[]{:S(2)}) copy-start(f32[270,270]{1,0:T(8,128)} %fusion.58) | copy-start | bytes 874804
  200.4 33.0 %copy-start.8 = (pred[270,270]{1,0:T(8,128)(4,1)S(1)}, pred[270,270]{1,0:T(8,128)(4,1)}, u32[]{:S(2)}) copy-start(pred[270,270]{1,0:T(8,128)(4,1)} %fusion.59) | copy-start | bytes 218704
  263.4 4.3 copy-start.1
  267.7 6.7 %copy-start.17 = (f32[4]{0:T(128)S(1)}, f32[4]{0:T(128)}, u32[]{:S(2)}) copy-start(f32[4]{0:T(128)} %get-tuple-element.552) | copy-start | bytes 52
  267.7 6.8 %copy-start.10 = (f32[4,16]{0,1:T(8,128)S(1)}, f32[4,16]{0,1:T(8,128)}, u32[]{:S(2)}) copy-start(f32[4,16]{0,1:T(8,128)} %get-tuple-element.563) | copy-start | bytes 772
  267.7 7.0 %copy-start.11 = (f32[4,270]{1,0:T(4,128)S(1)}, f32[4,270]{1,0:T(4,128)}, u32[]{:S(2)}) copy-start(f32[4,270]{1,0:T(4,128)} %get-tuple-element.565) | copy-start | bytes 12964
  295.1 5.6 copy-start.22
  295.1 127.3 %all-to-all-start.1 = ((f32[120,4,4320]{0,1,2:T(4,128)}), f32[120,4,4320]{0,1,2:T(4,128)}, u32[]{:S(2)}, u32[]{:S(2)}) async-start(f32[120,4,4320]{0,1,2:T(4,128)} %bitcast.111), calls=%async_computation.1 | async-start | bytes 17694720 | tf_op jit(solution)/shard_map/all_to_all | solution.py:142
  430.2 12.6 %copy-start.13 = (f32[64]{0:T(128)S(1)}, f32[64]{0:T(128)}, u32[]{:S(2)}) copy-start(f32[64]{0:T(128)} %copy-done.12) | copy-start | bytes 772
  430.2 12.6 %copy-start.15 = (f32[64]{0:T(128)S(1)}, f32[64]{0:T(128)}, u32[]{:S(2)}) copy-start(f32[64]{0:T(128)} %copy-done.14) | copy-start | bytes 772
  442.9 67.3 %copy-start.16 = (f32[64]{0:T(128)S(1)}, f32[64]{0:T(128)}, u32[]{:S(2)}) copy-start(f32[64]{0:T(128)} %get-tuple-element.551) | copy-start | bytes 772
  442.9 67.3 %copy-start.19 = (f32[64]{0:T(128)S(1)}, f32[64]{0:T(128)}, u32[]{:S(2)}) copy-start(f32[64]{0:T(128)} %get-tuple-element.562) | copy-start | bytes 772
  453.7 3.4 copy-start.4
  522.2 3.4 copy-start.3
  525.6 67.0 %copy-start.18 = (f32[64]{0:T(128)S(1)}, f32[64]{0:T(128)}, u32[]{:S(2)}) copy-start(f32[64]{0:T(128)} %get-tuple-element.550) | copy-start | bytes 772
  640.6 1.6 copy-start.5
  642.6 22.2 %collective-permute-start.1 = (f32[30,1,270]{2,1,0:T(1,128)S(1)}, f32[30,1,270]{2,1,0:T(1,128)S(1)}, u32[]{:S(2)}, u32[]{:S(2)}) collective-permute-start(f32[30,1,270]{2,1,0:T(1,128)S(1)} %get-tuple-element.557), channel_id=1, source_target_pairs={{0,16},{16,32},{32,48},{48,64},{64,80},{80,96},{96,112},{1,17},{17... | collective-permute-start | bytes 97208 | tf_op jit(solution)/shard_map/ppermute | solution.py:35
  644.3 20.5 %collective-permute-start = (f32[30,1,270]{2,1,0:T(1,128)S(1)}, f32[30,1,270]{2,1,0:T(1,128)S(1)}, u32[]{:S(2)}, u32[]{:S(2)}) collective-permute-start(f32[30,1,270]{2,1,0:T(1,128)S(1)} %get-tuple-element.556), channel_id=1, source_target_pairs={{16,0},{32,16},{48,32},{64,48},{80,64},{96,80},{112,96},{17,1},{33... | collective-permute-start | bytes 97208 | tf_op jit(solution)/shard_map/ppermute | solution.py:38
  646.1 16.0 %collective-permute-start.3 = (f32[30,64,1]{1,2,0:T(1,128)S(1)}, f32[30,64,1]{1,2,0:T(1,128)S(1)}, u32[]{:S(2)}, u32[]{:S(2)}) collective-permute-start(f32[30,64,1]{1,2,0:T(1,128)S(1)} %copy.159), channel_id=1, source_target_pairs={{0,1},{1,2},{2,3},{3,4},{4,5},{5,6},{6,7},{7,8},{8,9},{9,10},{10,1... | collective-permute-start | bytes 23048 | tf_op jit(solution)/shard_map/ppermute | solution.py:35
  646.5 16.9 %collective-permute-start.2 = (f32[30,64,1]{1,2,0:T(1,128)S(1)}, f32[30,64,1]{1,2,0:T(1,128)S(1)}, u32[]{:S(2)}, u32[]{:S(2)}) collective-permute-start(f32[30,64,1]{1,2,0:T(1,128)S(1)} %copy.157), channel_id=1, source_target_pairs={{1,0},{2,1},{3,2},{4,3},{5,4},{6,5},{7,6},{8,7},{9,8},{10,9},{11,1... | collective-permute-start | bytes 23048 | tf_op jit(solution)/shard_map/ppermute | solution.py:38
  652.0 12.8 %copy-start.6 = (f32[30,64,270]{2,1,0:T(8,128)S(1)}, f32[30,64,270]{2,1,0:T(8,128)}, u32[]{:S(2)}) copy-start(f32[30,64,270]{2,1,0:T(8,128)} %copy-done.5) | copy-start | bytes 6220804
where the time goes:
time: 685 us; the launch traced here: 673 us
  local copies, waits for them, and re-layouts  188 us (27%)
  blocking collectives  179 us (26%)
  matrix products  104 us (15%)
  waiting for transfers between devices  95.3 us (14%)
  other arithmetic  82.9 us (12%)
  starting transfers between devices  21.7 us (3%)
    unnamed x1, blocking collectives  109 us
    all_to_all x1, waiting for transfers between devices, body(): lax.all_to_all(masked_in, 'lon', split_axis=1, concat_axis=2, tiled=True)  95.3 us
    all_gather x2, blocking collectives, carried_in(): pieces = jax.tree.map(lambda part: lax.all_gather(part, axis), value)  70.2 us
    dot_general x2, matrix products, sector_sweep(): jnp.einsum('rjk,crbk->crbj', kernel, tiles, precision=lax.Precision.HIGHEST)  59.5 us
    mul x4, local copies, waits for them, and re-layouts, masked(): field_values.reshape(groups, levels, band_rows, sector) * weights[None]  40.6 us
    unnamed x52, local copies, waits for them, and re-layouts  29.9 us
    mul x2, other arithmetic, masked(): field_values.reshape(groups, levels, band_rows, sector) * weights[None]  25.6 us
    dot_general x2, matrix products, band_pass(): jnp.einsum('ik,ckj->cij', kernel, field_values, precision=lax.Precision.H...  22.8 us
  transfers between devices with their start and end apart: 6, of which 1 were waited for; matrix products, arithmetic and copies ran while one was open for 5% of the time, Pallas kernels for 0%

commit v1 on v0

v1 whole, which is shorter than its diff:
```python
import functools
import math

import jax
import jax.numpy as jnp
from jax import lax
from jax.experimental import pallas as pl
from jax.experimental.pallas import tpu as pltpu
from jax.sharding import PartitionSpec as P

COMP = 120
LEVELS = 30
ROWS = 64
SECTOR = 270
LANES = 128
BLOCKS = 3
TAIL = SECTOR - 2 * LANES
CLASSES = 16
PITCH = 136
PRESSURE_PITCH = 40
EXTENT = 272
PADDED = 320
BAND = 16
STRIP = 72
MESH = pl.DeviceIdType.MESH
F32 = jnp.float32
BF16 = jnp.bfloat16
SMEM = pl.BlockSpec(memory_space=pltpu.SMEM)
VMEM = pl.BlockSpec(memory_space=pltpu.VMEM)
LIMIT = 50 * 1024 * 1024


def lane_iota(rows):
    return lax.broadcasted_iota(jnp.int32, (rows, LANES), 1)


def lane_of(value, lane):
    return jnp.broadcast_to(value[:, lane : lane + 1], value.shape)


def class_decay(rate_ref):
    row = lax.broadcasted_iota(jnp.int32, (CLASSES, LANES), 0)
    decay = jnp.zeros((CLASSES, LANES), F32)
    for entry in range(CLASSES):
        decay = jnp.where(row == entry, rate_ref[entry], decay)
    return decay


def split(value):
    high = value.astype(BF16)
    return high, (value - high.astype(F32)).astype(BF16)


def transposed_dot(left, right):
    return lax.dot_general(left, right, (((1,), (1,)), ((), ())), preferred_element_type=F32)


def identity(size):
    shape = (size, size)
    same = lax.broadcasted_iota(jnp.int32, shape, 0) == lax.broadcasted_iota(jnp.int32, shape, 1)
    return same.astype(F32).astype(BF16)


def row_keep(class_ref, rate_ref, first, rows):
    at = lax.broadcasted_iota(jnp.int32, (rows, LANES), 0)
    decay = jnp.zeros((rows, LANES), F32)
    for k in range(rows):
        decay = jnp.where(at == k, rate_ref[class_ref[first + k]], decay)
    return 1.0 - decay


def longitude_kernel(
    class_ref, rate_ref, control_ref, mask_ref, y_ref, ew_ref, q_ref, weight_ref, edge_ref, rim_ref, flat, sea
):
    step = pl.program_id(0)

    @pl.when(step == 0)
    def _():
        flat[...] = jnp.zeros_like(flat)

    lane = lane_iota(8)
    for level in range(LEVELS):
        for part in range(BAND // 8):
            for block in range(BLOCKS):
                weight = mask_ref[level, part * 8 : part * 8 + 8, pl.ds(block * LANES, LANES)].astype(F32)
                if block == BLOCKS - 1:
                    weight = jnp.where(lane < TAIL, weight, 0.0)
                for group in range(4):
                    place = part * 8 * PITCH + group * LEVELS + level
                    flat[block, pl.ds(place, 8, stride=PITCH), :] = weight

    eye = identity(2 * LANES)
    small = eye[:16, :LANES]

    def pair(k, _):
        at = [pl.ds(pl.multiple_of((2 * k + n) * PITCH, 8), LANES) for n in range(2)]
        parts = [
            jnp.concatenate([flat[b, at[n], :] for n in range(2)], axis=0).astype(BF16)
            for b in range(BLOCKS)
        ]
        main = transposed_dot(eye, jnp.concatenate(parts[:2], axis=1))
        tail = transposed_dot(small, parts[2])
        for n in range(2):
            whole = jnp.concatenate(
                [main[:, n * LANES : (n + 1) * LANES], tail[:, n * LANES : (n + 1) * LANES]], axis=0
            )
            row = 2 * k + n
            weight_ref[row] = whole.astype(BF16)
            for t in range(EXTENT // 8):
                sea[pl.ds(t * 8 * BAND + row, 8, stride=BAND), :] = whole[t * 8 : t * 8 + 8]
        return 0

    lax.fori_loop(0, BAND // 2, pair, 0)

    @pl.when(step == 0)
    def _():
        rim_ref[0] = weight_ref[0].astype(F32)

    @pl.when(step == ROWS // BAND - 1)
    def _():
        rim_ref[1] = weight_ref[BAND - 1].astype(F32)

    edge_ref[0] = sea[:BAND]
    edge_ref[1] = sea[(SECTOR - 1) * BAND : SECTOR * BAND]

    keep = row_keep(class_ref, rate_ref, step * BAND, BAND)
    q = keep * keep
    q4 = q * q
    q8 = q4 * q4
    q256 = q8
    for _ in range(5):
        q256 = q256 * q256
    q_ref[...] = q256 * q8 * q4 * q

    def taken(j):
        inside = sea[pl.ds(pl.multiple_of(j * BAND, BAND), BAND), :] != 0.0
        return jnp.where(inside, control_ref[j], 0.0)

    def early(k, carried):
        east, west = carried
        back = SECTOR - 1 - k
        east = keep * east + taken(k)
        y_ref[k] = east
        held = keep * west
        y_ref[back] = held
        return east, held + taken(back)

    def late(k, carried):
        east, west = carried
        back = SECTOR - 1 - k
        east = keep * east + taken(k)
        y_ref[k] = y_ref[k] + east
        held = keep * west
        y_ref[back] = y_ref[back] + held
        return east, held + taken(back)

    zero = jnp.zeros((BAND, LANES), F32)
    half = SECTOR // 2
    carried = lax.fori_loop(0, half, early, (zero, zero), unroll=5)
    east, west = lax.fori_loop(half, SECTOR, late, carried, unroll=5)
    y_ref[SECTOR] = keep * east
    y_ref[SECTOR + 1] = keep * west
    for part in range(BAND // 8):
        ew_ref[2 * part] = east[part * 8 : part * 8 + 8]
        ew_ref[2 * part + 1] = west[part * 8 : part * 8 + 8]


def lon_carry_kernel(ew_ref, q_ref, edge_ref, ab_ref, edges_ref, first, second, send_sem, first_sem, second_sem, edge_sem):
    lat, me, count = lax.axis_index("lat"), lax.axis_index("lon"), 16

    barrier = pltpu.get_barrier_semaphore()

    def greet(k, _):
        pl.semaphore_signal(barrier, inc=1, device_id=(lat, lax.rem(me + k, count)), device_id_type=MESH)
        return 0

    lax.fori_loop(1, count, greet, 0)
    pl.semaphore_wait(barrier, count - 1)

    def to_share(k):
        to = lax.rem(me + k, count)
        return pltpu.make_async_remote_copy(
            src_ref=ew_ref.at[to],
            dst_ref=first.at[me],
            send_sem=send_sem.at[to],
            recv_sem=first_sem.at[me],
            device_id=(lat, to),
            device_id_type=MESH,
        )

    def at_share(k):
        source = lax.rem(me + k, count)
        return pltpu.make_async_remote_copy(
            src_ref=first.at[source],
            dst_ref=first.at[source],
            send_sem=send_sem.at[source],
            recv_sem=first_sem.at[source],
            device_id=(lat, source),
            device_id_type=MESH,
        )

    def edge_copy(side):
        to = lax.rem(me + (count - 1 if side == 0 else 1), count)
        return pltpu.make_async_remote_copy(
            src_ref=edge_ref.at[side],
            dst_ref=edges_ref.at[1 - side],
            send_sem=edge_sem.at[side],
            recv_sem=edge_sem.at[2 + 1 - side],
            device_id=(lat, to),
            device_id_type=MESH,
        )

    lax.fori_loop(1, count, lambda k, c: (to_share(k).start(), c)[1], 0)
    edge_copy(0).start()
    edge_copy(1).start()
    first[me] = ew_ref[me]
    lax.fori_loop(1, count, lambda k, c: (at_share(k).wait_recv(), c)[1], 0)
    lax.fori_loop(1, count, lambda k, c: (to_share(k).wait_send(), c)[1], 0)

    q = q_ref[pl.ds(pl.multiple_of(me // 2 * 8, 8), 8)]
    is_east = jnp.full((8, LANES), me % 2) == 0
    zero = jnp.zeros((8, LANES), F32)
    ahead, behind = [zero], [zero]
    for t in range(count):
        ahead.append(q * ahead[-1] + first[t])
        behind.append(q * behind[-1] + first[count - 1 - t])
    whole = q
    for _ in range(4):
        whole = whole * whole
    closing = jnp.where(is_east, ahead[count], behind[count]) / (1.0 - whole)
    lift, lifts = jnp.ones((8, LANES), F32), []
    for t in range(count):
        lifts.append(lift)
        lift = lift * q
    for t in range(count):
        opened = jnp.where(is_east, ahead[t], behind[count - 1 - t])
        raised = jnp.where(is_east, lifts[t], lifts[count - 1 - t])
        second[t] = opened + raised * closing

    def to_owner(k):
        to = lax.rem(me + k, count)
        return pltpu.make_async_remote_copy(
            src_ref=second.at[to],
            dst_ref=ab_ref.at[me],
            send_sem=send_sem.at[to],
            recv_sem=second_sem.at[me],
            device_id=(lat, to),
            device_id_type=MESH,
        )

    def at_owner(k):
        source = lax.rem(me + k, count)
        return pltpu.make_async_remote_copy(
            src_ref=second.at[source],
            dst_ref=ab_ref.at[source],
            send_sem=send_sem.at[source],
            recv_sem=second_sem.at[source],
            device_id=(lat, source),
            device_id_type=MESH,
        )

    lax.fori_loop(1, count, lambda k, c: (to_owner(k).start(), c)[1], 0)
    ab_ref[me] = second[me]
    lax.fori_loop(1, count, lambda k, c: (at_owner(k).wait_recv(), c)[1], 0)
    lax.fori_loop(1, count, lambda k, c: (to_owner(k).wait_send(), c)[1], 0)
    edge_copy(0).wait()
    edge_copy(1).wait()


def latitude_kernel(class_ref, rate_ref, y_ref, ab_ref, s_ref, closing_ref, response_ref, constants_ref, tables, drive):
    step = pl.program_id(0)
    tiles = STRIP // 8
    row_of = lax.broadcasted_iota(jnp.int32, (8, LANES), 0)
    decay = class_decay(rate_ref)
    log_keep = jnp.log(1.0 - decay)
    drive[...] = decay * jnp.sqrt(decay / (2.0 - decay))
    place = step * STRIP + lax.broadcasted_iota(jnp.int32, (STRIP, LANES), 0)
    ahead = jnp.where(place == SECTOR + 1, 0, place + 1).astype(F32)
    behind = jnp.where(place == SECTOR + 1, SECTOR + 1, jnp.maximum(SECTOR - place, 0)).astype(F32)
    for entry in range(CLASSES):
        tables[entry, 0] = jnp.exp(log_keep[entry : entry + 1] * ahead)
        tables[entry, 1] = jnp.exp(log_keep[entry : entry + 1] * behind)

    def forward(row, carried):
        north, unit = carried[:tiles], carried[tiles]
        entry = class_ref[row]
        keep = 1.0 - rate_ref[entry]
        gain = jnp.broadcast_to(drive[pl.ds(entry, 1), :], (8, LANES))
        at = row // 8 * 2
        a = jnp.broadcast_to(ab_ref[at, pl.ds(row % 8, 1), :], (8, LANES))
        b = jnp.broadcast_to(ab_ref[at + 1, pl.ds(row % 8, 1), :], (8, LANES))
        done = []
        for t in range(tiles):
            rows = pl.ds(t * 8, 8)
            y = y_ref[pl.ds(t * 8 * ROWS + row, 8, stride=ROWS), :]
            y = y + a * tables[entry, 0, rows, :] + b * tables[entry, 1, rows, :]
            done.append(keep * north[t] + gain * y)
            s_ref[row, rows, :] = done[t]
        unit = keep * unit
        response_ref[0, pl.ds(row, 1), :] = unit[:1]
        return (*done, unit)

    zero = jnp.zeros((8, LANES), F32)
    ones = jnp.ones((8, LANES), F32)
    done = lax.fori_loop(0, ROWS, forward, (*[zero] * tiles, ones), unroll=4)
    for t in range(tiles):
        closing_ref[0, pl.ds(t * 8, 8), :] = done[t]
    product = done[tiles]

    def backward(k, carried):
        south, unit, inflow = carried[:tiles], carried[tiles], carried[tiles + 1]
        row = ROWS - 1 - k
        decay = rate_ref[class_ref[row]]
        keep = 1.0 - decay
        done = []
        for t in range(tiles):
            rows = pl.ds(t * 8, 8)
            done.append(keep * south[t] + decay * s_ref[row, rows, :])
            s_ref[row, rows, :] = done[t]
        unit = keep * unit + decay * jnp.broadcast_to(response_ref[0, pl.ds(row, 1), :], (8, LANES))
        inflow = keep * inflow
        response_ref[0, pl.ds(row, 1), :] = unit[:1]
        response_ref[1, pl.ds(row, 1), :] = inflow[:1]
        return (*done, unit, inflow)

    done = lax.fori_loop(0, ROWS, backward, (*[zero] * tiles, zero, ones), unroll=4)
    for t in range(tiles):
        closing_ref[1, pl.ds(t * 8, 8), :] = done[t]
    last = rate_ref[class_ref[ROWS - 1]]
    constants = jnp.where(row_of == 0, product, done[tiles])
    constants = jnp.where(row_of == 2, 1.0 - last, constants)
    constants_ref[...] = jnp.where(row_of == 3, last, constants)


def lat_carry_kernel(
    closing_ref, constants_ref, rim_ref, inflow_ref, below_ref, rims_ref,
    first, second, others, send_sem, first_sem, second_sem, rate_send, rate_sem, rim_sem,
):
    me, lon, count = lax.axis_index("lat"), lax.axis_index("lon"), 8
    share = PADDED // 8

    barrier = pltpu.get_barrier_semaphore()

    def greet(k, _):
        pl.semaphore_signal(barrier, inc=1, device_id=(lax.rem(me + k, count), lon), device_id_type=MESH)
        return 0

    lax.fori_loop(1, count, greet, 0)
    pl.semaphore_wait(barrier, count - 1)

    def part(index):
        return pl.ds(pl.multiple_of(index * share, share), share)

    def to_share(k):
        to = lax.rem(me + k, count)
        return pltpu.make_async_remote_copy(
            src_ref=closing_ref.at[:, part(to)],
            dst_ref=first.at[me],
            send_sem=send_sem.at[to],
            recv_sem=first_sem.at[me],
            device_id=(to, lon),
            device_id_type=MESH,
        )

    def at_share(k):
        source = lax.rem(me + k, count)
        return pltpu.make_async_remote_copy(
            src_ref=first.at[source],
            dst_ref=first.at[source],
            send_sem=send_sem.at[source],
            recv_sem=first_sem.at[source],
            device_id=(source, lon),
            device_id_type=MESH,
        )

    def rate_copy(k, slot):
        to = lax.rem(me + k, count)
        return pltpu.make_async_remote_copy(
            src_ref=constants_ref,
            dst_ref=others.at[slot],
            send_sem=rate_send.at[to],
            recv_sem=rate_sem.at[slot],
            device_id=(to, lon),
            device_id_type=MESH,
        )

    def rim_copy(side):
        to = lax.rem(me + (count - 1 if side == 0 else 1), count)
        return pltpu.make_async_remote_copy(
            src_ref=rim_ref.at[side],
            dst_ref=rims_ref.at[1 - side],
            send_sem=rim_sem.at[side],
            recv_sem=rim_sem.at[2 + 1 - side],
            device_id=(to, lon),
            device_id_type=MESH,
        )

    lax.fori_loop(1, count, lambda k, c: (rate_copy(k, me).start(), c)[1], 0)
    lax.fori_loop(1, count, lambda k, c: (to_share(k).start(), c)[1], 0)
    rim_copy(0).start()
    rim_copy(1).start()
    first[me] = closing_ref[:, part(me)]
    others[me] = constants_ref[...]
    lax.fori_loop(1, count, lambda k, c: (rate_copy(k, lax.rem(me + k, count)).wait_recv(), c)[1], 0)
    lax.fori_loop(1, count, lambda k, c: (at_share(k).wait_recv(), c)[1], 0)
    lax.fori_loop(1, count, lambda k, c: (rate_copy(k, me).wait_send(), c)[1], 0)
    lax.fori_loop(1, count, lambda k, c: (to_share(k).wait_send(), c)[1], 0)

    shape = (share, LANES)
    second[0, 0] = jnp.zeros(shape, F32)
    for t in range(count - 1):
        second[t + 1, 0] = first[t, 0] + others[t, 0:1, :] * second[t, 0]
    second[count - 1, 1] = jnp.zeros(shape, F32)
    for t in range(count - 1, 0, -1):
        second[t - 1, 1] = (
            first[t, 1] + others[t, 1:2, :] * second[t, 0] + others[t, 0:1, :] * second[t, 1]
        )

    def to_owner(k):
        to = lax.rem(me + k, count)
        return pltpu.make_async_remote_copy(
            src_ref=second.at[to],
            dst_ref=inflow_ref.at[:, part(me)],
            send_sem=send_sem.at[to],
            recv_sem=second_sem.at[me],
            device_id=(to, lon),
            device_id_type=MESH,
        )

    def at_owner(k):
        source = lax.rem(me + k, count)
        return pltpu.make_async_remote_copy(
            src_ref=second.at[source],
            dst_ref=inflow_ref.at[:, part(source)],
            send_sem=send_sem.at[source],
            recv_sem=second_sem.at[source],
            device_id=(source, lon),
            device_id_type=MESH,
        )

    lax.fori_loop(1, count, lambda k, c: (to_owner(k).start(), c)[1], 0)
    inflow_ref[:, part(me)] = second[me]
    below = others[lax.rem(me + count - 1, count)]
    below_ref[...] = below * (me > 0).astype(F32)
    lax.fori_loop(1, count, lambda k, c: (at_owner(k).wait_recv(), c)[1], 0)
    lax.fori_loop(1, count, lambda k, c: (to_owner(k).wait_send(), c)[1], 0)
    rim_copy(0).wait()
    rim_copy(1).wait()


def final_kernel(
    s_ref, weight_ref, mask_ref, inflow_ref, response_ref, below_ref, rims_ref, edges_ref, balance_ref,
    increment_ref, velocity_ref, mixer, picker, padded, mixed, sea, pressure, kept, factor,
):
    step = pl.program_id(0)
    lane = lane_iota(8)

    @pl.when(step == 0)
    def _():
        padded[...] = jnp.zeros_like(padded)
        padded[:COMP, :COMP] = balance_ref[...]
        high, low = split(padded[:LANES])
        mixer[:LANES, :LANES] = high
        mixer[:LANES, LANES:] = high
        mixer[LANES:, :LANES] = low
        mixer[LANES:, LANES:] = jnp.zeros_like(low)
        high, low = split(padded[COMP - LEVELS : COMP - LEVELS + 32])
        picker[:32, :LANES] = high
        picker[:32, LANES:] = high
        picker[32:, :LANES] = low
        picker[32:, LANES:] = jnp.zeros_like(low)
        row = lax.axis_index("lat") * ROWS + lax.broadcasted_iota(jnp.int32, (ROWS, LANES), 0)
        latitude = (-70.0 + 140.0 * (row.astype(F32) + 0.5) / 512.0) * (math.pi / 180.0)
        sine = jnp.sin(latitude)
        factor[...] = 0.5 * (sine / (sine * sine + 0.01))

    def operand(field):
        high, low = split(field)
        return jnp.concatenate([high, low], axis=1)

    def pressures(both):
        product = transposed_dot(picker[...], both)
        total = product[:32] + product[32:]
        end = jnp.concatenate([total[:, 2 * LANES :], jnp.zeros((32, 3 * LANES - EXTENT), F32)], axis=1)
        return [total[:, :LANES], total[:, LANES : 2 * LANES], end]

    def rim_row(field, side, row):
        rim = rims_ref[side]
        result = pressures(operand(field * rim))
        shown = transposed_dot(identity(LANES)[:32], rim.astype(BF16))
        shown = jnp.concatenate([shown, jnp.zeros((32, 3 * LANES - EXTENT), F32)], axis=1)
        for b in range(BLOCKS):
            pressure[b, row * PRESSURE_PITCH : row * PRESSURE_PITCH + 32, :] = (
                result[b] * shown[:, b * LANES : (b + 1) * LANES]
            )

    @pl.when(step == 0)
    def _():
        north, south = inflow_ref[0, :EXTENT], inflow_ref[1, :EXTENT]
        first = s_ref[0] + response_ref[0, 0:1, :] * north + response_ref[1, 0:1, :] * south
        rim_row(below_ref[2:3, :] * first + below_ref[3:4, :] * north, 0, 0)

    @pl.when(step == ROWS // 8)
    def _():
        rim_row(inflow_ref[1, :EXTENT], 1, ROWS + 1)

    @pl.when(step < ROWS // 8)
    def _():
        rows = pl.ds(pl.multiple_of(step * 8, 8), 8)
        west, east = edges_ref[0, rows], edges_ref[1, rows]
        for level in range(LEVELS):
            for block in range(BLOCKS):
                weight = mask_ref[level, :, pl.ds(block * LANES, LANES)].astype(F32)
                if block == BLOCKS - 1:
                    weight = jnp.where(lane == TAIL, lane_of(east, level), weight)
                    weight = jnp.where(lane == TAIL + 1, lane_of(west, level), weight)
                sea[block, pl.ds(level, 8, stride=PRESSURE_PITCH), :] = weight

        def one_row(i, _):
            row = step * 8 + i
            h, p = response_ref[0, pl.ds(row, 1), :], response_ref[1, pl.ds(row, 1), :]
            tail = lax.broadcasted_iota(jnp.int32, (8, LANES), 0)
            weight = weight_ref[i].astype(F32)
            e, w = edges_ref[1, pl.ds(row, 1), :], edges_ref[0, pl.ds(row, 1), :]
            end = jnp.where(tail == 6, e, jnp.where(tail == 7, w, weight[EXTENT - 8 :]))
            weight = jnp.concatenate([weight[: EXTENT - 8], end], axis=0)
            field = s_ref[i] + h * inflow_ref[0, :EXTENT] + p * inflow_ref[1, :EXTENT]
            both = operand(field * weight)
            product = transposed_dot(both, mixer[...])
            total = (product[:, :LANES] + product[:, LANES:]) * weight
            for t in range(EXTENT // 8):
                mixed[pl.ds(t * 64 + i, 8, stride=8), :] = total[t * 8 : t * 8 + 8]
            result = pressures(both)
            at = pl.multiple_of((row + 1) * PRESSURE_PITCH, 8)
            for b in range(BLOCKS):
                pressure[b, pl.ds(at, 32), :] = (
                    result[b] * sea[b, pl.ds(pl.multiple_of(i * PRESSURE_PITCH, 8), 32), :]
                )
            return 0

        lax.fori_loop(0, 8, one_row, 0)

        def place(j, _):
            increment_ref[j] = mixed[pl.ds(pl.multiple_of(j * 8, 8), 8), :]
            return 0

        lax.fori_loop(0, SECTOR, place, 0, unroll=10)

    @pl.when(step > 0)
    def _():
        done = step - 1
        base = done * (8 * PRESSURE_PITCH)
        scale = factor[pl.ds(pl.multiple_of(done * 8, 8), 8)]
        for level in range(LEVELS):
            centre = []
            for block in range(BLOCKS):
                below, here, above = [
                    pressure[block, pl.ds(base + k * PRESSURE_PITCH + level, 8, stride=PRESSURE_PITCH), :]
                    for k in range(3)
                ]
                centre.append(here)
                weight = kept[level, :, pl.ds(block * LANES, LANES)].astype(F32)
                velocity_ref[0, level, :, pl.ds(block * LANES, LANES)] = (
                    -scale * (above - below) * weight
                )
            ups = [pltpu.roll(c, LANES - 1, 1) for c in centre]
            downs = [pltpu.roll(c, 1, 1) for c in centre]
            wrap = pltpu.roll(centre[2], LANES - TAIL - 1, 1)
            for block in range(BLOCKS):
                right = ups[block]
                if block < BLOCKS - 1:
                    right = jnp.where(lane == LANES - 1, ups[block + 1], right)
                left = jnp.where(lane == 0, downs[block - 1] if block else wrap, downs[block])
                weight = kept[level, :, pl.ds(block * LANES, LANES)].astype(F32)
                velocity_ref[1, level, :, pl.ds(block * LANES, LANES)] = (
                    scale * (right - left) * weight
                )

    @pl.when(step < ROWS // 8)
    def _():
        kept[...] = mask_ref[...]


def body(control, land_mask, row_class, decay_rate, balance):
    wide = BLOCKS * LANES
    params = functools.partial(pltpu.CompilerParams, vmem_limit_bytes=LIMIT)

    def like(*shape, dtype=F32):
        return jax.ShapeDtypeStruct(shape, dtype)

    columns = jnp.transpose(control, (2, 1, 0))
    y, ew, q, weight, edge, rim = pl.pallas_call(
        longitude_kernel,
        grid=(ROWS // BAND,),
        in_specs=[
            SMEM,
            SMEM,
            pl.BlockSpec((SECTOR, BAND, LANES), lambda g: (0, g, 0)),
            pl.BlockSpec((LEVELS, BAND, wide), lambda g: (0, g, 0)),
        ],
        out_specs=[
            pl.BlockSpec((EXTENT, BAND, LANES), lambda g: (0, g, 0)),
            pl.BlockSpec((BAND // 4, 8, LANES), lambda g: (g, 0, 0)),
            pl.BlockSpec((BAND, LANES), lambda g: (g, 0)),
            pl.BlockSpec((BAND, EXTENT, LANES), lambda g: (g, 0, 0)),
            pl.BlockSpec((2, BAND, LANES), lambda g: (0, g, 0)),
            pl.BlockSpec((2, EXTENT, LANES), lambda g: (0, 0, 0)),
        ],
        out_shape=[
            like(EXTENT, ROWS, LANES),
            like(16, 8, LANES),
            like(ROWS, LANES),
            like(ROWS, EXTENT, LANES, dtype=BF16),
            like(2, ROWS, LANES),
            like(2, EXTENT, LANES),
        ],
        scratch_shapes=[
            pltpu.VMEM((BLOCKS, BAND * PITCH, LANES), F32),
            pltpu.VMEM((EXTENT * BAND, LANES), F32),
        ],
        compiler_params=params(),
        name="longitude",
    )(row_class, decay_rate, columns, land_mask)

    ab, edges = pl.pallas_call(
        lon_carry_kernel,
        in_specs=[VMEM, VMEM, VMEM],
        out_specs=[VMEM, VMEM],
        out_shape=[like(16, 8, LANES), like(2, ROWS, LANES)],
        scratch_shapes=[
            pltpu.VMEM((16, 8, LANES), F32),
            pltpu.VMEM((16, 8, LANES), F32),
            pltpu.SemaphoreType.DMA((16,)),
            pltpu.SemaphoreType.DMA((16,)),
            pltpu.SemaphoreType.DMA((16,)),
            pltpu.SemaphoreType.DMA((4,)),
        ],
        compiler_params=params(collective_id=0, has_side_effects=True),
        name="lon_carry",
    )(ew, q, edge)

    s, closing, response, constants = pl.pallas_call(
        latitude_kernel,
        grid=(pl.cdiv(EXTENT, STRIP),),
        in_specs=[
            SMEM,
            SMEM,
            pl.BlockSpec((STRIP * ROWS, LANES), lambda g: (g, 0)),
            VMEM,
        ],
        out_specs=[
            pl.BlockSpec((ROWS, STRIP, LANES), lambda g: (0, g, 0)),
            pl.BlockSpec((2, STRIP, LANES), lambda g: (0, g, 0)),
            pl.BlockSpec((2, ROWS, LANES), lambda g: (0, 0, 0)),
            pl.BlockSpec((8, LANES), lambda g: (0, 0)),
        ],
        out_shape=[
            like(ROWS, EXTENT, LANES),
            like(2, PADDED, LANES),
            like(2, ROWS, LANES),
            like(8, LANES),
        ],
        scratch_shapes=[
            pltpu.VMEM((CLASSES, 2, STRIP, LANES), F32),
            pltpu.VMEM((CLASSES, LANES), F32),
        ],
        compiler_params=params(),
        name="latitude",
    )(row_class, decay_rate, y.reshape(EXTENT * ROWS, LANES), ab)

    share = PADDED // 8
    inflow, below, rims = pl.pallas_call(
        lat_carry_kernel,
        in_specs=[VMEM, VMEM, VMEM],
        out_specs=[VMEM, VMEM, VMEM],
        out_shape=[like(2, PADDED, LANES), like(8, LANES), like(2, EXTENT, LANES)],
        scratch_shapes=[
            pltpu.VMEM((8, 2, share, LANES), F32),
            pltpu.VMEM((8, 2, share, LANES), F32),
            pltpu.VMEM((8, 8, LANES), F32),
            pltpu.SemaphoreType.DMA((8,)),
            pltpu.SemaphoreType.DMA((8,)),
            pltpu.SemaphoreType.DMA((8,)),
            pltpu.SemaphoreType.DMA((8,)),
            pltpu.SemaphoreType.DMA((8,)),
            pltpu.SemaphoreType.DMA((4,)),
        ],
        compiler_params=params(collective_id=1, has_side_effects=True),
        name="lat_carry",
    )(closing, constants, rim)

    increment, velocity = pl.pallas_call(
        final_kernel,
        grid=(ROWS // 8 + 1,),
        in_specs=[
            pl.BlockSpec((8, EXTENT, LANES), lambda g: (jnp.minimum(g, 7), 0, 0)),
            pl.BlockSpec((8, EXTENT, LANES), lambda g: (jnp.minimum(g, 7), 0, 0)),
            pl.BlockSpec((LEVELS, 8, wide), lambda g: (0, jnp.minimum(g, 7), 0)),
            *[VMEM] * 6,
        ],
        out_specs=[
            pl.BlockSpec((SECTOR, 8, LANES), lambda g: (0, jnp.minimum(g, 7), 0)),
            pl.BlockSpec((2, LEVELS, 8, wide), lambda g: (0, 0, jnp.maximum(g - 1, 0), 0)),
        ],
        out_shape=[like(SECTOR, ROWS, COMP), like(2, LEVELS, ROWS, SECTOR)],
        scratch_shapes=[
            pltpu.VMEM((2 * LANES, 2 * LANES), BF16),
            pltpu.VMEM((64, 2 * LANES), BF16),
            pltpu.VMEM((LANES, LANES), F32),
            pltpu.VMEM((EXTENT * 8, LANES), F32),
            pltpu.VMEM((BLOCKS, 8 * PRESSURE_PITCH, LANES), F32),
            pltpu.VMEM((BLOCKS, (ROWS + 2) * PRESSURE_PITCH, LANES), F32),
            pltpu.VMEM((LEVELS, 8, wide), jnp.int32),
            pltpu.VMEM((ROWS, LANES), F32),
        ],
        compiler_params=params(),
        name="final",
    )(s, weight, land_mask, inflow, response, below, rims, edges, balance)
    return jnp.transpose(increment, (2, 1, 0)), velocity


def solution(mesh):
    return jax.shard_map(
        body,
        mesh=mesh,
        in_specs=(P(None, "lat", "lon"), P(None, "lat", "lon"), P("lat"), P(), P()),
        out_specs=(P(None, "lat", "lon"), P(None, None, "lat", "lon")),
        check_vma=False,
    )
```

time: 685 us -> 103 us (0.15); the launches traced: 673 us -> 103 us
  local copies, waits for them, and re-layouts: 188 us -> 3.14 us
  blocking collectives: 179 us -> 0 us
  matrix products: 104 us -> 0 us
  Pallas kernels: 0 us -> 99.3 us
  waiting for transfers between devices: 95.3 us -> 0 us
  other arithmetic: 82.9 us -> 0 us
  starting transfers between devices: 21.7 us -> 0 us
    unnamed x1 -> x0, blocking collectives: 109 us -> none
    dot_general x5 -> x0, matrix products: 104 us -> none  [the longest x2 59.5 us: sector_sweep(): jnp.einsum('rjk,crbk->crbj', kernel, tiles, precision=lax.Precision.HIGHEST)]
    pallas_call x0 -> x5, Pallas kernels: none -> 99.3 us  [the longest x1 26.5 us: body(): pl.pallas_call(final_kernel, grid=(ROWS // 8 + 1,), in_specs=[pl.BlockSpe...]
    all_to_all x2 -> x0, waiting for transfers between devices: 95.3 us -> none  [the longest x1 95.3 us: body(): lax.all_to_all(masked_in, 'lon', split_axis=1, concat_axis=2, tiled=True)]
    all_gather x2 -> x0, blocking collectives: 70.2 us -> none  [carried_in(): pieces = jax.tree.map(lambda part: lax.all_gather(part, axis), value)]
    mul x4 -> x0, local copies, waits for them, and re-layouts: 40.6 us -> none  [masked(): field_values.reshape(groups, levels, band_rows, sector) * weights[None]]
    dynamic_slice x62 -> x0, local copies, waits for them, and re-layouts: 32.4 us -> none  [the longest x28 19.6 us: step(): longer = join(running, jax.tree.map(lambda part: part[position], pieces))]
    all_to_all x3 -> x0, local copies, waits for them, and re-layouts: 31.8 us -> none  [the longest x2 20.4 us: body(): lax.all_to_all(westward, 'lon', split_axis=2, concat_axis=1, tiled=True)]
  transfers between devices with their start and end apart: 6 -> 0, of which waited for: 1 -> 0; matrix products, arithmetic and copies ran while one was open for 5% -> 0% of each run, Pallas kernels for 0% -> 0%
where the time goes in v1:
time: 103 us
  Pallas kernels  99.3 us (96%)
  local copies, waits for them, and re-layouts  3.14 us (3%)
    pallas_call x1, Pallas kernels, body(): pl.pallas_call(final_kernel, grid=(ROWS // 8 + 1,), in_specs=[pl.BlockSpe...  26.5 us
    pallas_call x1, Pallas kernels, body(): pl.pallas_call(longitude_kernel, grid=(ROWS // BAND,), in_specs=[SMEM, SM...  20.7 us
    pallas_call x1, Pallas kernels, body(): pl.pallas_call(lat_carry_kernel, in_specs=[VMEM, VMEM, VMEM], out_specs=[...  19.1 us
    pallas_call x1, Pallas kernels, body(): pl.pallas_call(lon_carry_kernel, in_specs=[VMEM, VMEM, VMEM], out_specs=[...  16.9 us
    pallas_call x1, Pallas kernels, body(): pl.pallas_call(latitude_kernel, grid=(pl.cdiv(EXTENT, STRIP),), in_specs=...  16 us
    unnamed x10, local copies, waits for them, and re-layouts  3.14 us

profile of v1, /device:TPU:0, one launch (start us, length us, event | category | flops | bytes accessed | tf_op | source)
XLA Modules:
  0.0 103.1 jit_solution(6668843965787150132)
XLA Ops:
  0.6 0.0 copy-start
  0.6 1.8 %copy-done = s32[30,64,270]{2,1,0:T(8,128)S(1)} copy-done((s32[30,64,270]{2,1,0:T(8,128)S(1)}, s32[30,64,270]{2,1,0:T(8,128)}, u32[]{:S(2)}) %copy-start) | copy-done | bytes 2073624
  2.5 0.0 copy-start.3
  2.5 0.7 copy-done.3
  3.1 0.0 copy-start.4
  3.1 0.7 copy-done.4
  3.8 0.0 copy-start.1
  3.8 0.0 copy-start.2
  3.8 20.7 %longitude.1 = (f32[272,64,128]{2,1,0:T(8,128)}, f32[16,8,128]{2,1,0:T(8,128)S(1)}, f32[64,128]{1,0:T(8,128)S(1)}, bf16[64,272,128]{2,1,0:T(8,128)(2,1)}, f32[2,...) custom-call(s32[64]{0:T(128)S(1)} %copy-done.3, f32[16]{0:T(128)S(1)} %copy-done.4, f32[270,64,120]{2,1,0:T(8,128)} %bitcast.4, ...), custom_call_target="tpu_custom_call" | custom-call | tf_op jit(solution)/shard_map/longitude/pallas_call | solution.py:592
  24.5 16.9 %lon_carry.1 = (f32[16,8,128]{2,1,0:T(8,128)S(1)}, f32[2,64,128]{2,1,0:T(8,128)S(1)}) custom-call(f32[16,8,128]{2,1,0:T(8,128)S(1)} %get-tuple-element.20.ew_ref, f32[64,128]{1,0:T(8,128)S(1)} %get-tuple-element.21.q_ref, f32[2,64,128]{2,1,0:T(8,128)S(1)} %get-tuple-element.22.edge_ref), custom_call_target="tpu_custom_call" | custom-call | tf_op jit(solution)/shard_map/lon_carry/pallas_call | solution.py:625
  41.4 16.0 %latitude.1 = (f32[64,272,128]{2,1,0:T(8,128)}, f32[2,320,128]{2,1,0:T(8,128)S(1)}, f32[2,64,128]{2,1,0:T(8,128)S(1)}, f32[8,128]{1,0:T(8,128)S(1)}) custom-call(s32[64]{0:T(128)S(1)} %copy-done.3, f32[16]{0:T(128)S(1)} %copy-done.4, f32[17408,128]{1,0:T(8,128)} %bitcast.3, f32[16,8,128]{2,1,0:T(8,128)S(1)} %get-tuple-element.23.ab_ref), custom_call_target="tpu_custom_call" | custom-call | tf_op jit(solution)/shard_map/latitude/pallas_call | solution.py:642
  57.4 19.1 %lat_carry.1 = (f32[2,320,128]{2,1,0:T(8,128)S(1)}, f32[8,128]{1,0:T(8,128)S(1)}, f32[2,272,128]{2,1,0:T(8,128)S(1)}) custom-call(f32[2,320,128]{2,1,0:T(8,128)S(1)} %get-tuple-element.26.closing_ref, f32[8,128]{1,0:T(8,128)S(1)} %get-tuple-element.27.constants_ref, f32[2,272,128]{2,1,0:T(8,128)S(1)} %get-tuple-element.28.rim_ref), custom_call_target="tpu_custom_call" | custom-call | tf_op jit(solution)/shard_map/lat_carry/pallas_call | solution.py:672
  76.6 0.0 copy-done.1
  76.6 0.0 copy-done.2
  76.6 26.5 %final.1 = (f32[270,64,120]{2,1,0:T(8,128)}, f32[2,30,64,270]{3,2,1,0:T(8,128)}) custom-call(f32[64,272,128]{2,1,0:T(8,128)} %get-tuple-element.24.s_ref, bf16[64,272,128]{2,1,0:T(8,128)(2,1)} %get-tuple-element.25.weight_ref, s32[30,64,270]{2,1,0:T(8,128)S(1)} %copy-done.1, f32[2,320,128]{2,1,0:T(8,128)S(1)} %get-tuple-element.29.inflow_ref, ...), custom_call_target="tpu_custom_call" | custom-call | tf_op jit(solution)/shard_map/final/pallas_call | solution.py:692
Async XLA Ops:
  0.6 1.8 %copy-start = (s32[30,64,270]{2,1,0:T(8,128)S(1)}, s32[30,64,270]{2,1,0:T(8,128)}, u32[]{:S(2)}) copy-start(s32[30,64,270]{2,1,0:T(8,128)} %mask_ref.3) | copy-start | bytes 6220804
  2.5 0.7 copy-start.3
  3.1 0.7 copy-start.4
  3.8 72.8 %copy-start.1 = (s32[30,64,270]{2,1,0:T(8,128)S(1)}, s32[30,64,270]{2,1,0:T(8,128)}, u32[]{:S(2)}) copy-start(s32[30,64,270]{2,1,0:T(8,128)} %mask_ref.3) | copy-start | bytes 6220804
  3.8 72.8 %copy-start.2 = (f32[120,120]{1,0:T(8,128)S(1)}, f32[120,120]{1,0:T(8,128)}, u32[]{:S(2)}) copy-start(f32[120,120]{1,0:T(8,128)} %balance_ref.1) | copy-start | bytes 172804

commit v2 on v1

v2 whole, which is shorter than its diff:
```python
import functools
import math

import jax
import jax.numpy as jnp
from jax import lax
from jax.experimental import pallas as pl
from jax.experimental.pallas import tpu as pltpu
from jax.sharding import PartitionSpec as P

COMP = 120
LEVELS = 30
ROWS = 64
SECTOR = 270
LANES = 128
BLOCKS = 3
TAIL = SECTOR - 2 * LANES
CLASSES = 16
PITCH = 136
PRESSURE_PITCH = 40
EXTENT = 272
BAND = 16
BANDS = ROWS // BAND
ROW_PITCH = 72
SEA_PITCH = 24
SHARE = 40
TILES = SHARE // 8
SHARES = 7
PADDED = SHARES * SHARE
LON = 16
LAT = 8
MESH = pl.DeviceIdType.MESH
F32 = jnp.float32
BF16 = jnp.bfloat16
SMEM = pl.BlockSpec(memory_space=pltpu.SMEM)
VMEM = pl.BlockSpec(memory_space=pltpu.VMEM)
LIMIT = 58 * 1024 * 1024


def lane_iota(rows):
    return lax.broadcasted_iota(jnp.int32, (rows, LANES), 1)


def lane_of(value, lane):
    return jnp.broadcast_to(value[:, lane : lane + 1], value.shape)


def class_decay(rate_ref):
    row = lax.broadcasted_iota(jnp.int32, (CLASSES, LANES), 0)
    decay = jnp.zeros((CLASSES, LANES), F32)
    for entry in range(CLASSES):
        decay = jnp.where(row == entry, rate_ref[entry], decay)
    return decay


def split(value):
    high = value.astype(BF16)
    return high, (value - high.astype(F32)).astype(BF16)


def transposed_dot(left, right):
    return lax.dot_general(left, right, (((1,), (1,)), ((), ())), preferred_element_type=F32)


def identity(size):
    shape = (size, size)
    same = lax.broadcasted_iota(jnp.int32, shape, 0) == lax.broadcasted_iota(jnp.int32, shape, 1)
    return same.astype(F32).astype(BF16)


def row_keep(class_ref, rate_ref, first, rows):
    at = lax.broadcasted_iota(jnp.int32, (rows, LANES), 0)
    decay = jnp.zeros((rows, LANES), F32)
    for k in range(rows):
        decay = jnp.where(at == k, rate_ref[class_ref[first + k]], decay)
    return 1.0 - decay


def analysis_kernel(
    class_ref, rate_ref, control_ref, mask_ref,
    weight_ref, s_ref, inflow_ref, response_ref, below_ref, rims_ref, edges_ref,
    flat, sea, columns, field, state, closing, keeps, laps, starts, rates,
    ew, first, second, ab, edge, edges_in, rim, rims_in, constants, others, lat_first, lat_second, inflow_in,
    ew_send, first_sem, second_send, second_sem, edge_send, edge_sem, rim_send, rim_sem,
    rate_send, rate_sem, share_send, share_sem, reply_send, reply_sem, out_sem,
):
    step = pl.program_id(0)
    lat, lon = lax.axis_index("lat"), lax.axis_index("lon")
    barrier = pltpu.get_barrier_semaphore()

    def remote(source, target, send, recv, to):
        return pltpu.make_async_remote_copy(
            src_ref=source, dst_ref=target, send_sem=send, recv_sem=recv, device_id=to, device_id_type=MESH
        )

    def lon_peer(k):
        return lax.rem(lon + k, LON)

    def lat_peer(k):
        return lax.rem(lat + k, LAT)

    def each(count, act):
        lax.fori_loop(1, count, lambda k, c: (act(k), c)[1], 0)

    def closing_copy(index, slot):
        return remote(ew.at[index], first.at[slot], ew_send.at[index], first_sem.at[slot], (lat, index))

    def carry_copy(to, slot):
        return remote(second.at[to], ab.at[slot], second_send.at[to], second_sem.at[slot], (lat, to))

    def edge_copy(side):
        to = lon_peer(LON - 1 if side == 0 else 1)
        return remote(edge.at[side], edges_in.at[1 - side], edge_send.at[side], edge_sem.at[1 - side], (lat, to))

    def rim_copy(side):
        to = lat_peer(LAT - 1 if side == 0 else 1)
        return remote(rim.at[side], rims_in.at[1 - side], rim_send.at[side], rim_sem.at[1 - side], (to, lon))

    def rate_copy(to, slot):
        return remote(constants, others.at[slot], rate_send.at[to], rate_sem.at[slot], (to, lon))

    def part(index):
        return pl.ds(pl.multiple_of(index * SHARE, 8), SHARE)

    def share_copy(index, slot):
        return remote(
            closing.at[:, part(index)], lat_first.at[slot], share_send.at[index], share_sem.at[slot], (index, lon)
        )

    def share_arrival(slot):
        return remote(lat_first.at[slot], lat_first.at[slot], share_send.at[slot], share_sem.at[slot], (slot, lon))

    def reply_copy(to, index):
        return remote(
            lat_second.at[to], inflow_in.at[:, part(index)], reply_send.at[to], reply_sem.at[index], (to, lon)
        )

    def out_copy(index):
        return pltpu.make_async_copy(field.at[:, part(index)], s_ref.at[:, part(index)], out_sem.at[index])

    zero = jnp.zeros((8, LANES), F32)
    ones = jnp.ones((8, LANES), F32)

    @pl.when(step == 0)
    def _():
        each(LON, lambda k: pl.semaphore_signal(barrier, inc=1, device_id=(lat, lon_peer(k)), device_id_type=MESH))
        each(LAT, lambda k: pl.semaphore_signal(barrier, inc=1, device_id=(lat_peer(k), lon), device_id_type=MESH))
        flat[...] = jnp.zeros_like(flat)
        columns[EXTENT * ROW_PITCH :] = jnp.zeros(((PADDED - EXTENT) * ROW_PITCH, LANES), F32)
        state[...] = jnp.zeros_like(state)
        for block in range(ROWS // 8):
            keep = row_keep(class_ref, rate_ref, block * 8, 8)
            keeps[block * 8 : block * 8 + 8] = keep
            q = keep * keep
            q4 = q * q
            q8 = q4 * q4
            q256 = q8
            for _ in range(5):
                q256 = q256 * q256
            laps[block * 8 : block * 8 + 8] = q256 * q8 * q4 * q
        decay = class_decay(rate_ref)
        log_keep = jnp.log(1.0 - decay)
        rates[0] = decay * jnp.sqrt(decay / (2.0 - decay))
        rates[1] = jnp.exp(log_keep * 8.0)
        rates[2] = jnp.exp(log_keep * (SECTOR + 1.0))
        row = lax.broadcasted_iota(jnp.int32, (8, LANES), 0).astype(F32)
        for entry in range(CLASSES):
            log = log_keep[entry : entry + 1]
            for index in range(SHARES):
                starts[index, entry, 0] = jnp.exp(log * (row + (SHARE * index + 1.0)))
                starts[index, entry, 1] = jnp.exp(log * (SECTOR + 8.0 - SHARE * (index + 1.0) - row))

        def onward(i, unit):
            unit = jnp.broadcast_to(keeps[pl.ds(i, 1), :], (8, LANES)) * unit
            response_ref[0, pl.ds(i, 1), :] = unit[:1]
            return unit

        product = lax.fori_loop(0, ROWS, onward, ones, unroll=4)

        def back(k, carried):
            unit, inflow = carried
            i = ROWS - 1 - k
            keep = jnp.broadcast_to(keeps[pl.ds(i, 1), :], (8, LANES))
            unit = keep * unit + (1.0 - keep) * jnp.broadcast_to(response_ref[0, pl.ds(i, 1), :], (8, LANES))
            inflow = keep * inflow
            response_ref[0, pl.ds(i, 1), :] = unit[:1]
            response_ref[1, pl.ds(i, 1), :] = inflow[:1]
            return unit, inflow

        unit, _ = lax.fori_loop(0, ROWS, back, (zero, ones), unroll=4)
        at = lax.broadcasted_iota(jnp.int32, (8, LANES), 0)
        last = jnp.broadcast_to(keeps[ROWS - 1 :], (8, LANES))
        tile = jnp.where(at == 0, product, unit)
        tile = jnp.where(at == 2, last, tile)
        constants[...] = jnp.where(at == 3, 1.0 - last, tile)

    lane = lane_iota(8)
    for level in range(LEVELS):
        for half in range(BAND // 8):
            for block in range(BLOCKS):
                weight = mask_ref[level, half * 8 : half * 8 + 8, pl.ds(block * LANES, LANES)].astype(F32)
                if block == BLOCKS - 1:
                    weight = jnp.where(lane < TAIL, weight, 0.0)
                for group in range(4):
                    place = half * 8 * PITCH + group * LEVELS + level
                    flat[block, pl.ds(place, 8, stride=PITCH), :] = weight

    eye = identity(2 * LANES)
    small = eye[:16, :LANES]

    def pair(k, _):
        at = [pl.ds(pl.multiple_of((2 * k + n) * PITCH, 8), LANES) for n in range(2)]
        parts = [
            jnp.concatenate([flat[b, at[n], :] for n in range(2)], axis=0).astype(BF16)
            for b in range(BLOCKS)
        ]
        main = transposed_dot(eye, jnp.concatenate(parts[:2], axis=1))
        tail = transposed_dot(small, parts[2])
        for n in range(2):
            whole = jnp.concatenate(
                [main[:, n * LANES : (n + 1) * LANES], tail[:, n * LANES : (n + 1) * LANES]], axis=0
            )
            row = 2 * k + n
            weight_ref[row] = whole.astype(BF16)
            for t in range(EXTENT // 8):
                sea[pl.ds(t * 8 * SEA_PITCH + row, 8, stride=SEA_PITCH), :] = whole[t * 8 : t * 8 + 8]
        return 0

    lax.fori_loop(0, BAND // 2, pair, 0, unroll=4)

    here = pl.ds(pl.multiple_of(step * BAND, BAND), BAND)
    edge[0, here] = sea[:BAND]
    edge[1, here] = sea[(SECTOR - 1) * SEA_PITCH : (SECTOR - 1) * SEA_PITCH + BAND]

    keep = keeps[here]
    keep2 = keep * keep

    def taken(j):
        inside = sea[pl.ds(pl.multiple_of(j * SEA_PITCH, 8), BAND), :] != 0.0
        return jnp.where(inside, control_ref[j], 0.0)

    def spot(j):
        return pl.ds(pl.multiple_of(j * ROW_PITCH + step * BAND, 8), BAND)

    def advance(p, carried, add_east, add_west):
        east, west = carried
        j, k = 2 * p, SECTOR - 1 - 2 * p
        x0, x1 = taken(j), taken(j + 1)
        z0, z1 = taken(k), taken(k - 1)
        mid = keep * x0 + x1
        e0 = keep * east + x0
        e1 = keep2 * east + mid
        if add_east:
            columns[spot(j)] = columns[spot(j)] + e0
            columns[spot(j + 1)] = columns[spot(j + 1)] + e1
        else:
            columns[spot(j)] = e0
            columns[spot(j + 1)] = e1
        w0 = keep * west
        w1 = keep2 * west + keep * z0
        if add_west:
            columns[spot(k)] = columns[spot(k)] + w0
            columns[spot(k - 1)] = columns[spot(k - 1)] + w1
        else:
            columns[spot(k)] = w0
            columns[spot(k - 1)] = w1
        return e1, keep2 * west + (keep * z0 + z1)

    nothing = jnp.zeros((BAND, LANES), F32)
    pairs = SECTOR // 2
    carried = lax.fori_loop(
        0, pairs // 2 - 1, lambda p, c: advance(p, c, False, False), (nothing, nothing), unroll=3
    )
    carried = advance(pairs // 2 - 1, carried, False, False)
    carried = advance(pairs // 2, carried, False, True)
    carried = lax.fori_loop(
        pairs // 2 + 1, pairs - 1, lambda p, c: advance(p, c, True, True), carried, unroll=3
    )
    east, west = advance(pairs - 1, carried, True, True)
    columns[spot(SECTOR)] = keep * east
    columns[spot(SECTOR + 1)] = keep * west

    @pl.when(step == 0)
    def _():
        rim[0] = weight_ref[0].astype(F32)
        pl.semaphore_wait(barrier, LON + LAT - 2)
        each(LAT, lambda k: rate_copy(lat_peer(k), lat).start())
        others[lat] = constants[...]
        rim_copy(0).start()

    for half in range(BAND // 8):
        for side, value in enumerate((east, west)):
            index = step * 4 + half * 2 + side
            ew[index] = value[half * 8 : half * 8 + 8]

            @pl.when(index != lon)
            def _():
                closing_copy(index, lon).start()

            @pl.when(index == lon)
            def _():
                first[lon] = value[half * 8 : half * 8 + 8]

    @pl.when(step == BANDS - 1)
    def _():
        rim[1] = weight_ref[BAND - 1].astype(F32)
        edge_copy(0).start()
        edge_copy(1).start()
        rim_copy(1).start()

    owner = lon // 4

    @pl.when((owner == step - 1) | ((step == BANDS - 1) & (owner == step)))
    def _():
        each(LON, lambda k: closing_copy(lon_peer(k), lon_peer(k)).wait_recv())
        q = laps[pl.ds(pl.multiple_of(lon // 2 * 8, 8), 8)]
        is_east = jnp.full((8, LANES), lon % 2) == 0
        ahead, behind = [zero], [zero]
        for t in range(LON):
            ahead.append(q * ahead[-1] + first[t])
            behind.append(q * behind[-1] + first[LON - 1 - t])
        whole = q
        for _ in range(4):
            whole = whole * whole
        end = jnp.where(is_east, ahead[LON], behind[LON]) / (1.0 - whole)
        lift, lifts = ones, []
        for t in range(LON):
            lifts.append(lift)
            lift = lift * q
        for t in range(LON):
            opened = jnp.where(is_east, ahead[t], behind[LON - 1 - t])
            raised = jnp.where(is_east, lifts[t], lifts[LON - 1 - t])
            second[t] = opened + raised * end
        each(LON, lambda k: carry_copy(lon_peer(k), lon).start())
        ab[lon] = second[lon]

    special = lax.broadcasted_iota(jnp.int32, (8, LANES), 0) == 7

    def forward_band(band, _):
        def arrive(n, c):
            index = band * 4 + n

            @pl.when(index != lon)
            def _():
                carry_copy(index, index).wait_recv()

            return c

        lax.fori_loop(0, 4, arrive, 0)

        def strip(index, _):
            final = special & (jnp.full((8, LANES), index) == SHARES - 1)
            base = pl.multiple_of(index * SHARE, 8)

            def one_row(ii, north):
                row = band * BAND + ii
                entry = class_ref[row]
                keep = 1.0 - rate_ref[entry]
                gain, stride8, far = [
                    jnp.broadcast_to(rates[n, pl.ds(entry, 1), :], (8, LANES)) for n in range(3)
                ]
                at = row // 8 * 2
                a = jnp.broadcast_to(ab[at, pl.ds(row % 8, 1), :], (8, LANES))
                b = jnp.broadcast_to(ab[at + 1, pl.ds(row % 8, 1), :], (8, LANES))
                ahead = [a * starts[index, entry, 0]]
                behind = [b * starts[index, entry, 1]]
                for _ in range(TILES - 1):
                    ahead.append(ahead[-1] * stride8)
                    behind.append(behind[-1] * stride8)
                behind = behind[::-1]
                ahead[3] = jnp.where(final, a, ahead[3])
                behind[3] = jnp.where(final, b * far, behind[3])
                done = []
                for t in range(TILES):
                    y = columns[pl.ds((base + t * 8) * ROW_PITCH + row, 8, stride=ROW_PITCH), :]
                    done.append(keep * north[t] + gain * (y + ahead[t] + behind[t]))
                    field[row, pl.ds(base + t * 8, 8), :] = done[t]
                return tuple(done)

            north = tuple(state[pl.ds(base + t * 8, 8), :] for t in range(TILES))
            north = lax.fori_loop(0, BAND, one_row, north, unroll=4)
            for t in range(TILES):
                state[pl.ds(base + t * 8, 8), :] = north[t]
            return 0

        lax.fori_loop(0, SHARES, strip, 0)
        return 0

    lax.fori_loop(
        jnp.where(step == BANDS - 1, 1, 0),
        jnp.where(step == BANDS - 1, BANDS, jnp.where(step == BANDS - 2, 1, 0)),
        forward_band,
        0,
    )

    @pl.when(step == BANDS - 1)
    def _():
        closing[0] = state[...]
        each(LAT, lambda k: rate_copy(lat_peer(k), lat_peer(k)).wait_recv())

        def strip(index, _):
            base = pl.multiple_of(index * SHARE, 8)

            def one_row(k, south):
                row = ROWS - 1 - k
                decay = rate_ref[class_ref[row]]
                keep = 1.0 - decay
                done = []
                for t in range(TILES):
                    at = pl.ds(base + t * 8, 8)
                    done.append(keep * south[t] + decay * field[row, at, :])
                    field[row, at, :] = done[t]
                return tuple(done)

            south = lax.fori_loop(0, ROWS, one_row, (zero,) * TILES, unroll=4)
            for t in range(TILES):
                closing[1, pl.ds(base + t * 8, 8), :] = south[t]
            out_copy(index).start()

            @pl.when(index != lat)
            def _():
                share_copy(index, lat).start()

            @pl.when(index == lat)
            def _():
                lat_first[lat] = closing[:, part(lat)]

            @pl.when((lat < SHARES) & (index == jnp.minimum(lat + 2, SHARES - 1)))
            def _():
                each(LAT, lambda k: share_arrival(lat_peer(k)).wait_recv())
                blank = jnp.zeros((SHARE, LANES), F32)
                lat_second[0, 0] = blank
                for t in range(LAT - 1):
                    lat_second[t + 1, 0] = lat_first[t, 0] + others[t, 0:1, :] * lat_second[t, 0]
                lat_second[LAT - 1, 1] = blank
                for t in range(LAT - 1, 0, -1):
                    lat_second[t - 1, 1] = (
                        lat_first[t, 1]
                        + others[t, 1:2, :] * lat_second[t, 0]
                        + others[t, 0:1, :] * lat_second[t, 1]
                    )
                each(LAT, lambda k: reply_copy(lat_peer(k), lat).start())
                inflow_in[:, part(lat)] = lat_second[lat]

            return 0

        lax.fori_loop(0, SHARES, strip, 0)
        edge_copy(0).wait()
        edge_copy(1).wait()
        rim_copy(0).wait()
        rim_copy(1).wait()
        edges_ref[...] = edges_in[...]
        rims_ref[...] = rims_in[...]
        below_ref[...] = others[lat_peer(LAT - 1)] * (lat > 0).astype(F32)
        each(LON, lambda k: closing_copy(lon_peer(k), lon).wait_send())
        each(LON, lambda k: carry_copy(lon_peer(k), lon).wait_send())
        each(LAT, lambda k: rate_copy(lat_peer(k), lat).wait_send())

        def settle(index, c):
            @pl.when(index != lat)
            def _():
                share_copy(index, lat).wait_send()
                reply_copy(index, index).wait_recv()

            out_copy(index).wait()
            return c

        lax.fori_loop(0, SHARES, settle, 0)

        @pl.when(lat < SHARES)
        def _():
            each(LAT, lambda k: reply_copy(lat_peer(k), lat).wait_send())

        inflow_ref[...] = inflow_in[...]


def final_kernel(
    s_ref, weight_ref, mask_ref, inflow_ref, response_ref, below_ref, rims_ref, edges_ref, balance_ref,
    increment_ref, velocity_ref, mixer, picker, padded, mixed, sea, pressure, kept, factor,
):
    step = pl.program_id(0)
    lane = lane_iota(8)

    @pl.when(step == 0)
    def _():
        padded[...] = jnp.zeros_like(padded)
        padded[:COMP, :COMP] = balance_ref[...]
        high, low = split(padded[:LANES])
        mixer[:LANES, :LANES] = high
        mixer[:LANES, LANES:] = high
        mixer[LANES:, :LANES] = low
        mixer[LANES:, LANES:] = jnp.zeros_like(low)
        high, low = split(padded[COMP - LEVELS : COMP - LEVELS + 32])
        picker[:32, :LANES] = high
        picker[:32, LANES:] = high
        picker[32:, :LANES] = low
        picker[32:, LANES:] = jnp.zeros_like(low)
        row = lax.axis_index("lat") * ROWS + lax.broadcasted_iota(jnp.int32, (ROWS, LANES), 0)
        latitude = (-70.0 + 140.0 * (row.astype(F32) + 0.5) / 512.0) * (math.pi / 180.0)
        sine = jnp.sin(latitude)
        factor[...] = 0.5 * (sine / (sine * sine + 0.01))

    def operand(field):
        high, low = split(field)
        return jnp.concatenate([high, low], axis=1)

    def pressures(both):
        product = transposed_dot(picker[...], both)
        total = product[:32] + product[32:]
        end = jnp.concatenate([total[:, 2 * LANES :], jnp.zeros((32, 3 * LANES - EXTENT), F32)], axis=1)
        return [total[:, :LANES], total[:, LANES : 2 * LANES], end]

    def rim_row(field, side, row):
        rim = rims_ref[side]
        result = pressures(operand(field * rim))
        shown = transposed_dot(identity(LANES)[:32], rim.astype(BF16))
        shown = jnp.concatenate([shown, jnp.zeros((32, 3 * LANES - EXTENT), F32)], axis=1)
        for b in range(BLOCKS):
            pressure[b, row * PRESSURE_PITCH : row * PRESSURE_PITCH + 32, :] = (
                result[b] * shown[:, b * LANES : (b + 1) * LANES]
            )

    @pl.when(step == 0)
    def _():
        north, south = inflow_ref[0, :EXTENT], inflow_ref[1, :EXTENT]
        first = s_ref[0] + response_ref[0, 0:1, :] * north + response_ref[1, 0:1, :] * south
        rim_row(below_ref[2:3, :] * first + below_ref[3:4, :] * north, 0, 0)

    @pl.when(step == ROWS // 8)
    def _():
        rim_row(inflow_ref[1, :EXTENT], 1, ROWS + 1)

    @pl.when(step < ROWS // 8)
    def _():
        rows = pl.ds(pl.multiple_of(step * 8, 8), 8)
        west, east = edges_ref[0, rows], edges_ref[1, rows]
        for level in range(LEVELS):
            for block in range(BLOCKS):
                weight = mask_ref[level, :, pl.ds(block * LANES, LANES)].astype(F32)
                if block == BLOCKS - 1:
                    weight = jnp.where(lane == TAIL, lane_of(east, level), weight)
                    weight = jnp.where(lane == TAIL + 1, lane_of(west, level), weight)
                sea[block, pl.ds(level, 8, stride=PRESSURE_PITCH), :] = weight

        def one_row(i, _):
            row = step * 8 + i
            h, p = response_ref[0, pl.ds(row, 1), :], response_ref[1, pl.ds(row, 1), :]
            tail = lax.broadcasted_iota(jnp.int32, (8, LANES), 0)
            weight = weight_ref[i].astype(F32)
            e, w = edges_ref[1, pl.ds(row, 1), :], edges_ref[0, pl.ds(row, 1), :]
            end = jnp.where(tail == 6, e, jnp.where(tail == 7, w, weight[EXTENT - 8 :]))
            weight = jnp.concatenate([weight[: EXTENT - 8], end], axis=0)
            field = s_ref[i] + h * inflow_ref[0, :EXTENT] + p * inflow_ref[1, :EXTENT]
            both = operand(field * weight)
            product = transposed_dot(both, mixer[...])
            total = (product[:, :LANES] + product[:, LANES:]) * weight
            for t in range(EXTENT // 8):
                mixed[pl.ds(t * 64 + i, 8, stride=8), :] = total[t * 8 : t * 8 + 8]
            result = pressures(both)
            at = pl.multiple_of((row + 1) * PRESSURE_PITCH, 8)
            for b in range(BLOCKS):
                pressure[b, pl.ds(at, 32), :] = (
                    result[b] * sea[b, pl.ds(pl.multiple_of(i * PRESSURE_PITCH, 8), 32), :]
                )
            return 0

        lax.fori_loop(0, 8, one_row, 0, unroll=4)

        def place(j, _):
            increment_ref[j] = mixed[pl.ds(pl.multiple_of(j * 8, 8), 8), :]
            return 0

        lax.fori_loop(0, SECTOR, place, 0, unroll=10)

    @pl.when(step > 0)
    def _():
        done = step - 1
        base = done * (8 * PRESSURE_PITCH)
        scale = factor[pl.ds(pl.multiple_of(done * 8, 8), 8)]
        for level in range(LEVELS):
            centre = []
            for block in range(BLOCKS):
                below, here, above = [
                    pressure[block, pl.ds(base + k * PRESSURE_PITCH + level, 8, stride=PRESSURE_PITCH), :]
                    for k in range(3)
                ]
                centre.append(here)
                weight = kept[level, :, pl.ds(block * LANES, LANES)].astype(F32)
                velocity_ref[0, level, :, pl.ds(block * LANES, LANES)] = (
                    -scale * (above - below) * weight
                )
            ups = [pltpu.roll(c, LANES - 1, 1) for c in centre]
            downs = [pltpu.roll(c, 1, 1) for c in centre]
            wrap = pltpu.roll(centre[2], LANES - TAIL - 1, 1)
            for block in range(BLOCKS):
                right = ups[block]
                if block < BLOCKS - 1:
                    right = jnp.where(lane == LANES - 1, ups[block + 1], right)
                left = jnp.where(lane == 0, downs[block - 1] if block else wrap, downs[block])
                weight = kept[level, :, pl.ds(block * LANES, LANES)].astype(F32)
                velocity_ref[1, level, :, pl.ds(block * LANES, LANES)] = (
                    scale * (right - left) * weight
                )

    @pl.when(step < ROWS // 8)
    def _():
        kept[...] = mask_ref[...]


def body(control, land_mask, row_class, decay_rate, balance):
    wide = BLOCKS * LANES
    params = functools.partial(pltpu.CompilerParams, vmem_limit_bytes=LIMIT)

    def like(*shape, dtype=F32):
        return jax.ShapeDtypeStruct(shape, dtype)

    columns = jnp.transpose(control, (2, 1, 0))

    dma = pltpu.SemaphoreType.DMA
    fixed2, fixed3 = (lambda g: (0, 0)), (lambda g: (0, 0, 0))
    weight, s, inflow, response, below, rims, edges = pl.pallas_call(
        analysis_kernel,
        grid=(BANDS,),
        in_specs=[
            SMEM,
            SMEM,
            pl.BlockSpec((SECTOR, BAND, LANES), lambda g: (0, g, 0)),
            pl.BlockSpec((LEVELS, BAND, wide), lambda g: (0, g, 0)),
        ],
        out_specs=[
            pl.BlockSpec((BAND, EXTENT, LANES), lambda g: (g, 0, 0)),
            pl.BlockSpec(memory_space=pl.ANY),
            pl.BlockSpec((2, PADDED, LANES), fixed3),
            pl.BlockSpec((2, ROWS, LANES), fixed3),
            pl.BlockSpec((8, LANES), fixed2),
            pl.BlockSpec((2, EXTENT, LANES), fixed3),
            pl.BlockSpec((2, ROWS, LANES), fixed3),
        ],
        out_shape=[
            like(ROWS, EXTENT, LANES, dtype=BF16),
            like(ROWS, PADDED, LANES),
            like(2, PADDED, LANES),
            like(2, ROWS, LANES),
            like(8, LANES),
            like(2, EXTENT, LANES),
            like(2, ROWS, LANES),
        ],
        scratch_shapes=[
            pltpu.VMEM((BLOCKS, BAND * PITCH, LANES), F32),
            pltpu.VMEM((EXTENT * SEA_PITCH, LANES), F32),
            pltpu.VMEM((PADDED * ROW_PITCH, LANES), F32),
            pltpu.VMEM((ROWS, PADDED, LANES), F32),
            pltpu.VMEM((PADDED, LANES), F32),
            pltpu.VMEM((2, PADDED, LANES), F32),
            pltpu.VMEM((ROWS, LANES), F32),
            pltpu.VMEM((ROWS, LANES), F32),
            pltpu.VMEM((SHARES, CLASSES, 2, 8, LANES), F32),
            pltpu.VMEM((3, CLASSES, LANES), F32),
            pltpu.VMEM((LON, 8, LANES), F32),
            pltpu.VMEM((LON, 8, LANES), F32),
            pltpu.VMEM((LON, 8, LANES), F32),
            pltpu.VMEM((LON, 8, LANES), F32),
            pltpu.VMEM((2, ROWS, LANES), F32),
            pltpu.VMEM((2, ROWS, LANES), F32),
            pltpu.VMEM((2, EXTENT, LANES), F32),
            pltpu.VMEM((2, EXTENT, LANES), F32),
            pltpu.VMEM((8, LANES), F32),
            pltpu.VMEM((LAT, 8, LANES), F32),
            pltpu.VMEM((LAT, 2, SHARE, LANES), F32),
            pltpu.VMEM((LAT, 2, SHARE, LANES), F32),
            pltpu.VMEM((2, PADDED, LANES), F32),
            dma((LON,)),
            dma((LON,)),
            dma((LON,)),
            dma((LON,)),
            dma((2,)),
            dma((2,)),
            dma((2,)),
            dma((2,)),
            dma((LAT,)),
            dma((LAT,)),
            dma((LAT,)),
            dma((LAT,)),
            dma((LAT,)),
            dma((LAT,)),
            dma((SHARES,)),
        ],
        compiler_params=params(collective_id=0, has_side_effects=True),
        name="analysis",
    )(row_class, decay_rate, columns, land_mask)

    increment, velocity = pl.pallas_call(
        final_kernel,
        grid=(ROWS // 8 + 1,),
        in_specs=[
            pl.BlockSpec((8, EXTENT, LANES), lambda g: (jnp.minimum(g, 7), 0, 0)),
            pl.BlockSpec((8, EXTENT, LANES), lambda g: (jnp.minimum(g, 7), 0, 0)),
            pl.BlockSpec((LEVELS, 8, wide), lambda g: (0, jnp.minimum(g, 7), 0)),
            *[VMEM] * 6,
        ],
        out_specs=[
            pl.BlockSpec((SECTOR, 8, LANES), lambda g: (0, jnp.minimum(g, 7), 0)),
            pl.BlockSpec((2, LEVELS, 8, wide), lambda g: (0, 0, jnp.maximum(g - 1, 0), 0)),
        ],
        out_shape=[like(SECTOR, ROWS, COMP), like(2, LEVELS, ROWS, SECTOR)],
        scratch_shapes=[
            pltpu.VMEM((2 * LANES, 2 * LANES), BF16),
            pltpu.VMEM((64, 2 * LANES), BF16),
            pltpu.VMEM((LANES, LANES), F32),
            pltpu.VMEM((EXTENT * 8, LANES), F32),
            pltpu.VMEM((BLOCKS, 8 * PRESSURE_PITCH, LANES), F32),
            pltpu.VMEM((BLOCKS, (ROWS + 2) * PRESSURE_PITCH, LANES), F32),
            pltpu.VMEM((LEVELS, 8, wide), jnp.int32),
            pltpu.VMEM((ROWS, LANES), F32),
        ],
        compiler_params=params(),
        name="final",
    )(s, weight, land_mask, inflow, response, below, rims, edges, balance)
    return jnp.transpose(increment, (2, 1, 0)), velocity


def solution(mesh):
    return jax.shard_map(
        body,
        mesh=mesh,
        in_specs=(P(None, "lat", "lon"), P(None, "lat", "lon"), P("lat"), P(), P()),
        out_specs=(P(None, "lat", "lon"), P(None, None, "lat", "lon")),
        check_vma=False,
    )
```

time: 103 us -> 84.3 us (0.82)
  Pallas kernels: 99.3 us -> 83 us
  local copies, waits for them, and re-layouts: 3.14 us -> 0 us
    pallas_call x4 -> x1, Pallas kernels: 72.8 us -> 64.1 us  [body(): pl.pallas_call(analysis_kernel, grid=(BANDS,), in_specs=[SMEM, SMEM, pl.B...]
    pallas_call x1, Pallas kernels: 26.5 us -> 18.9 us  [body(): pl.pallas_call(final_kernel, grid=(ROWS // 8 + 1,), in_specs=[pl.BlockSpe...]
    unnamed x10 -> x0, local copies, waits for them, and re-layouts: 3.14 us -> none
where the time goes in v2:
time: 84.3 us; the launch traced here: 83.6 us
  Pallas kernels  83 us (98%)
    pallas_call x1, Pallas kernels, body(): pl.pallas_call(analysis_kernel, grid=(BANDS,), in_specs=[SMEM, SMEM, pl.B...  64.1 us
    pallas_call x1, Pallas kernels, body(): pl.pallas_call(final_kernel, grid=(ROWS // 8 + 1,), in_specs=[pl.BlockSpe...  18.9 us

profile of v2, /device:TPU:0, one launch (start us, length us, event | category | flops | bytes accessed | tf_op | source)
XLA Modules:
  0.0 83.6 jit_solution(490723241929604458)
XLA Ops:
  0.6 64.1 %analysis.1 = (bf16[64,272,128]{2,1,0:T(8,128)(2,1)}, f32[64,280,128]{2,1,0:T(8,128)}, f32[2,280,128]{2,1,0:T(8,128)}, f32[2,64,128]{2,1,0:T(8,128)}, f32[8,128]...) custom-call(s32[64]{0:T(128)} %class_ref.1, f32[16]{0:T(128)} %rate_ref.1, f32[270,64,120]{2,1,0:T(8,128)} %bitcast.2, ...), custom_call_target="tpu_custom_call" | custom-call | tf_op jit(solution)/shard_map/analysis/pallas_call | solution.py:621
  64.7 18.9 %final.1 = (f32[270,64,120]{2,1,0:T(8,128)}, f32[2,30,64,270]{3,2,1,0:T(8,128)}) custom-call(f32[64,280,128]{2,1,0:T(8,128)} %get-tuple-element.11.s_ref, bf16[64,272,128]{2,1,0:T(8,128)(2,1)} %get-tuple-element.12.weight_ref, s32[30,64,270]{2,1,0:T(8,128)} %mask_ref.3, f32[2,280,128]{2,1,0:T(8,128)} %get-tuple-element.13.inflow_ref, ...), custom_call_target="tpu_custom_call" | custom-call | tf_op jit(solution)/shard_map/final/pallas_call | solution.py:692

commit v3 on v2

--- a/solution.py
+++ b/solution.py
@@ -80,8 +80,8 @@
     class_ref, rate_ref, control_ref, mask_ref,
     weight_ref, s_ref, inflow_ref, response_ref, below_ref, rims_ref, edges_ref,
     flat, sea, columns, field, state, closing, keeps, laps, starts, rates,
-    ew, first, second, ab, edge, edges_in, rim, rims_in, constants, others, lat_first, lat_second, inflow_in,
-    ew_send, first_sem, second_send, second_sem, edge_send, edge_sem, rim_send, rim_sem,
+    ew, gathered, ab, edge, edges_in, rim, rims_in, constants, others, lat_first, lat_second, inflow_in,
+    ew_send, ew_sem, edge_send, edge_sem, rim_send, rim_sem,
     rate_send, rate_sem, share_send, share_sem, reply_send, reply_sem, out_sem,
 ):
     step = pl.program_id(0)
@@ -102,11 +102,8 @@
     def each(count, act):
         lax.fori_loop(1, count, lambda k, c: (act(k), c)[1], 0)
 
-    def closing_copy(index, slot):
-        return remote(ew.at[index], first.at[slot], ew_send.at[index], first_sem.at[slot], (lat, index))
-
-    def carry_copy(to, slot):
-        return remote(second.at[to], ab.at[slot], second_send.at[to], second_sem.at[slot], (lat, to))
+    def closing_copy(band, to, slot):
+        return remote(ew.at[band], gathered.at[band, slot], ew_send.at[band, to], ew_sem.at[band, slot], (lat, to))
 
     def edge_copy(side):
         to = lon_peer(LON - 1 if side == 0 else 1)
@@ -290,16 +287,9 @@
 
     for half in range(BAND // 8):
         for side, value in enumerate((east, west)):
-            index = step * 4 + half * 2 + side
-            ew[index] = value[half * 8 : half * 8 + 8]
-
-            @pl.when(index != lon)
-            def _():
-                closing_copy(index, lon).start()
-
-            @pl.when(index == lon)
-            def _():
-                first[lon] = value[half * 8 : half * 8 + 8]
+            ew[step, 2 * half + side] = value[half * 8 : half * 8 + 8]
+    each(LON, lambda k: closing_copy(step, lon_peer(k), lon).start())
+    gathered[step, lon] = ew[step]
 
     @pl.when(step == BANDS - 1)
     def _():
@@ -308,45 +298,26 @@
         edge_copy(1).start()
         rim_copy(1).start()
 
-    owner = lon // 4
-
-    @pl.when((owner == step - 1) | ((step == BANDS - 1) & (owner == step)))
-    def _():
-        each(LON, lambda k: closing_copy(lon_peer(k), lon_peer(k)).wait_recv())
-        q = laps[pl.ds(pl.multiple_of(lon // 2 * 8, 8), 8)]
-        is_east = jnp.full((8, LANES), lon % 2) == 0
-        ahead, behind = [zero], [zero]
-        for t in range(LON):
-            ahead.append(q * ahead[-1] + first[t])
-            behind.append(q * behind[-1] + first[LON - 1 - t])
-        whole = q
-        for _ in range(4):
-            whole = whole * whole
-        end = jnp.where(is_east, ahead[LON], behind[LON]) / (1.0 - whole)
-        lift, lifts = ones, []
-        for t in range(LON):
-            lifts.append(lift)
-            lift = lift * q
-        for t in range(LON):
-            opened = jnp.where(is_east, ahead[t], behind[LON - 1 - t])
-            raised = jnp.where(is_east, lifts[t], lifts[LON - 1 - t])
-            second[t] = opened + raised * end
-        each(LON, lambda k: carry_copy(lon_peer(k), lon).start())
-        ab[lon] = second[lon]
-
     special = lax.broadcasted_iota(jnp.int32, (8, LANES), 0) == 7
 
     def forward_band(band, _):
-        def arrive(n, c):
-            index = band * 4 + n
-
-            @pl.when(index != lon)
-            def _():
-                carry_copy(index, index).wait_recv()
-
-            return c
-
-        lax.fori_loop(0, 4, arrive, 0)
+        each(LON, lambda k: closing_copy(band, lon_peer(k), lon_peer(k)).wait_recv())
+        for half in range(BAND // 8):
+            q = laps[pl.ds(pl.multiple_of(band * BAND + half * 8, 8), 8)]
+            whole = q
+            for _ in range(4):
+                whole = whole * whole
+            part_of = 1.0 / (1.0 - whole)
+
+            def gather(k, carried):
+                a, b = carried
+                a = q * a + gathered[band, lon_peer(k), 2 * half]
+                b = q * b + gathered[band, lon_peer(LON - k), 2 * half + 1]
+                return a, b
+
+            a, b = lax.fori_loop(0, LON, gather, (zero, zero), unroll=4)
+            ab[2 * half] = a * part_of
+            ab[2 * half + 1] = b * part_of
 
         def strip(index, _):
             final = special & (jnp.full((8, LANES), index) == SHARES - 1)
@@ -359,7 +330,7 @@
                 gain, stride8, far = [
                     jnp.broadcast_to(rates[n, pl.ds(entry, 1), :], (8, LANES)) for n in range(3)
                 ]
-                at = row // 8 * 2
+                at = ii // 8 * 2
                 a = jnp.broadcast_to(ab[at, pl.ds(row % 8, 1), :], (8, LANES))
                 b = jnp.broadcast_to(ab[at + 1, pl.ds(row % 8, 1), :], (8, LANES))
                 ahead = [a * starts[index, entry, 0]]
@@ -386,19 +357,14 @@
         lax.fori_loop(0, SHARES, strip, 0)
         return 0
 
-    lax.fori_loop(
-        jnp.where(step == BANDS - 1, 1, 0),
-        jnp.where(step == BANDS - 1, BANDS, jnp.where(step == BANDS - 2, 1, 0)),
-        forward_band,
-        0,
-    )
-
     @pl.when(step == BANDS - 1)
     def _():
+        lax.fori_loop(0, BANDS, forward_band, 0)
         closing[0] = state[...]
         each(LAT, lambda k: rate_copy(lat_peer(k), lat_peer(k)).wait_recv())
 
-        def strip(index, _):
+        def strip(turn, _):
+            index = lax.rem(lat + turn, SHARES)
             base = pl.multiple_of(index * SHARE, 8)
 
             def one_row(k, south):
@@ -425,7 +391,7 @@
             def _():
                 lat_first[lat] = closing[:, part(lat)]
 
-            @pl.when((lat < SHARES) & (index == jnp.minimum(lat + 2, SHARES - 1)))
+            @pl.when((lat < SHARES) & (turn == SHARES - 1))
             def _():
                 each(LAT, lambda k: share_arrival(lat_peer(k)).wait_recv())
                 blank = jnp.zeros((SHARE, LANES), F32)
@@ -452,8 +418,8 @@
         edges_ref[...] = edges_in[...]
         rims_ref[...] = rims_in[...]
         below_ref[...] = others[lat_peer(LAT - 1)] * (lat > 0).astype(F32)
-        each(LON, lambda k: closing_copy(lon_peer(k), lon).wait_send())
-        each(LON, lambda k: carry_copy(lon_peer(k), lon).wait_send())
+        for band in range(BANDS):
+            each(LON, lambda k: closing_copy(band, lon_peer(k), lon).wait_send())
         each(LAT, lambda k: rate_copy(lat_peer(k), lat).wait_send())
 
         def settle(index, c):
@@ -656,10 +622,9 @@
             pltpu.VMEM((ROWS, LANES), F32),
             pltpu.VMEM((SHARES, CLASSES, 2, 8, LANES), F32),
             pltpu.VMEM((3, CLASSES, LANES), F32),
-            pltpu.VMEM((LON, 8, LANES), F32),
-            pltpu.VMEM((LON, 8, LANES), F32),
-            pltpu.VMEM((LON, 8, LANES), F32),
-            pltpu.VMEM((LON, 8, LANES), F32),
+            pltpu.VMEM((BANDS, 4, 8, LANES), F32),
+            pltpu.VMEM((BANDS, LON, 4, 8, LANES), F32),
+            pltpu.VMEM((4, 8, LANES), F32),
             pltpu.VMEM((2, ROWS, LANES), F32),
             pltpu.VMEM((2, ROWS, LANES), F32),
             pltpu.VMEM((2, EXTENT, LANES), F32),
@@ -669,10 +634,8 @@
             pltpu.VMEM((LAT, 2, SHARE, LANES), F32),
             pltpu.VMEM((LAT, 2, SHARE, LANES), F32),
             pltpu.VMEM((2, PADDED, LANES), F32),
-            dma((LON,)),
-            dma((LON,)),
-            dma((LON,)),
-            dma((LON,)),
+            dma((BANDS, LON)),
+            dma((BANDS, LON)),
             dma((2,)),
             dma((2,)),
             dma((2,)),

time: 84.3 us -> 66.3 us (0.79)
  Pallas kernels: 83 us -> 64.6 us
    pallas_call x1, Pallas kernels: 64.1 us -> 45.7 us  [body(): pl.pallas_call(analysis_kernel, grid=(BANDS,), in_specs=[SMEM, SMEM, pl.B...]
where the time goes in v3:
time: 66.3 us; the launch traced here: 65.2 us
  Pallas kernels  64.6 us (97%)
    pallas_call x1, Pallas kernels, body(): pl.pallas_call(analysis_kernel, grid=(BANDS,), in_specs=[SMEM, SMEM, pl.B...  45.7 us
    pallas_call x1, Pallas kernels, body(): pl.pallas_call(final_kernel, grid=(ROWS // 8 + 1,), in_specs=[pl.BlockSpe...  18.9 us

profile of v3, /device:TPU:0, one launch (start us, length us, event | category | flops | bytes accessed | tf_op | source)
XLA Modules:
  0.0 65.2 jit_solution(9272890180192738751)
XLA Ops:
  0.6 45.7 %analysis.1 = (bf16[64,272,128]{2,1,0:T(8,128)(2,1)}, f32[64,280,128]{2,1,0:T(8,128)}, f32[2,280,128]{2,1,0:T(8,128)}, f32[2,64,128]{2,1,0:T(8,128)}, f32[8,128]...) custom-call(s32[64]{0:T(128)} %class_ref.1, f32[16]{0:T(128)} %rate_ref.1, f32[270,64,120]{2,1,0:T(8,128)} %bitcast.2, ...), custom_call_target="tpu_custom_call" | custom-call | tf_op jit(solution)/shard_map/analysis/pallas_call | solution.py:587
  46.3 18.9 %final.1 = (f32[270,64,120]{2,1,0:T(8,128)}, f32[2,30,64,270]{3,2,1,0:T(8,128)}) custom-call(f32[64,280,128]{2,1,0:T(8,128)} %get-tuple-element.11.s_ref, bf16[64,272,128]{2,1,0:T(8,128)(2,1)} %get-tuple-element.12.weight_ref, s32[30,64,270]{2,1,0:T(8,128)} %mask_ref.3, f32[2,280,128]{2,1,0:T(8,128)} %get-tuple-element.13.inflow_ref, ...), custom_call_target="tpu_custom_call" | custom-call | tf_op jit(solution)/shard_map/final/pallas_call | solution.py:655

commit v4 on v3

--- a/solution.py
+++ b/solution.py
@@ -34,7 +34,7 @@
 BF16 = jnp.bfloat16
 SMEM = pl.BlockSpec(memory_space=pltpu.SMEM)
 VMEM = pl.BlockSpec(memory_space=pltpu.VMEM)
-LIMIT = 58 * 1024 * 1024
+LIMIT = 44 * 1024 * 1024
 
 
 def lane_iota(rows):
@@ -74,6 +74,23 @@
     for k in range(rows):
         decay = jnp.where(at == k, rate_ref[class_ref[first + k]], decay)
     return 1.0 - decay
+
+
+def widened(value):
+    return jnp.concatenate([value, jnp.zeros((value.shape[0], LANES - value.shape[1]), value.dtype)], axis=1)
+
+
+def block_of(ref, level, rows, block):
+    if block < BLOCKS - 1:
+        return ref[level, rows, pl.ds(block * LANES, LANES)]
+    return widened(ref[level, rows, pl.ds(block * LANES, TAIL)])
+
+
+def place_block(ref, side, level, block, value):
+    if block < BLOCKS - 1:
+        ref[side, level, :, pl.ds(block * LANES, LANES)] = value
+    else:
+        ref[side, level, :, pl.ds(block * LANES, TAIL)] = value[:, :TAIL]
 
 
 def analysis_kernel(
@@ -191,13 +208,10 @@
         tile = jnp.where(at == 2, last, tile)
         constants[...] = jnp.where(at == 3, 1.0 - last, tile)
 
-    lane = lane_iota(8)
     for level in range(LEVELS):
         for half in range(BAND // 8):
             for block in range(BLOCKS):
-                weight = mask_ref[level, half * 8 : half * 8 + 8, pl.ds(block * LANES, LANES)].astype(F32)
-                if block == BLOCKS - 1:
-                    weight = jnp.where(lane < TAIL, weight, 0.0)
+                weight = block_of(mask_ref, level, pl.ds(half * 8, 8), block).astype(F32)
                 for group in range(4):
                     place = half * 8 * PITCH + group * LEVELS + level
                     flat[block, pl.ds(place, 8, stride=PITCH), :] = weight
@@ -223,7 +237,7 @@
                 sea[pl.ds(t * 8 * SEA_PITCH + row, 8, stride=SEA_PITCH), :] = whole[t * 8 : t * 8 + 8]
         return 0
 
-    lax.fori_loop(0, BAND // 2, pair, 0, unroll=4)
+    lax.fori_loop(0, BAND // 2, pair, 0, unroll=8)
 
     here = pl.ds(pl.multiple_of(step * BAND, BAND), BAND)
     edge[0, here] = sea[:BAND]
@@ -234,7 +248,7 @@
 
     def taken(j):
         inside = sea[pl.ds(pl.multiple_of(j * SEA_PITCH, 8), BAND), :] != 0.0
-        return jnp.where(inside, control_ref[j], 0.0)
+        return jnp.where(inside, widened(control_ref[j]), 0.0)
 
     def spot(j):
         return pl.ds(pl.multiple_of(j * ROW_PITCH + step * BAND, 8), BAND)
@@ -349,7 +363,7 @@
                 return tuple(done)
 
             north = tuple(state[pl.ds(base + t * 8, 8), :] for t in range(TILES))
-            north = lax.fori_loop(0, BAND, one_row, north, unroll=4)
+            north = lax.fori_loop(0, BAND, one_row, north, unroll=16)
             for t in range(TILES):
                 state[pl.ds(base + t * 8, 8), :] = north[t]
             return 0
@@ -502,10 +516,11 @@
         west, east = edges_ref[0, rows], edges_ref[1, rows]
         for level in range(LEVELS):
             for block in range(BLOCKS):
-                weight = mask_ref[level, :, pl.ds(block * LANES, LANES)].astype(F32)
+                weight = block_of(mask_ref, level, pl.ds(0, 8), block).astype(F32)
                 if block == BLOCKS - 1:
                     weight = jnp.where(lane == TAIL, lane_of(east, level), weight)
                     weight = jnp.where(lane == TAIL + 1, lane_of(west, level), weight)
+                kept[step % 2, level, :, pl.ds(block * LANES, LANES)] = weight
                 sea[block, pl.ds(level, 8, stride=PRESSURE_PITCH), :] = weight
 
         def one_row(i, _):
@@ -530,10 +545,10 @@
                 )
             return 0
 
-        lax.fori_loop(0, 8, one_row, 0, unroll=4)
+        lax.fori_loop(0, 8, one_row, 0, unroll=8)
 
         def place(j, _):
-            increment_ref[j] = mixed[pl.ds(pl.multiple_of(j * 8, 8), 8), :]
+            increment_ref[j] = mixed[pl.ds(pl.multiple_of(j * 8, 8), 8), :COMP]
             return 0
 
         lax.fori_loop(0, SECTOR, place, 0, unroll=10)
@@ -551,10 +566,8 @@
                     for k in range(3)
                 ]
                 centre.append(here)
-                weight = kept[level, :, pl.ds(block * LANES, LANES)].astype(F32)
-                velocity_ref[0, level, :, pl.ds(block * LANES, LANES)] = (
-                    -scale * (above - below) * weight
-                )
+                weight = kept[(step + 1) % 2, level, :, pl.ds(block * LANES, LANES)]
+                place_block(velocity_ref, 0, level, block, -scale * (above - below) * weight)
             ups = [pltpu.roll(c, LANES - 1, 1) for c in centre]
             downs = [pltpu.roll(c, 1, 1) for c in centre]
             wrap = pltpu.roll(centre[2], LANES - TAIL - 1, 1)
@@ -563,22 +576,16 @@
                 if block < BLOCKS - 1:
                     right = jnp.where(lane == LANES - 1, ups[block + 1], right)
                 left = jnp.where(lane == 0, downs[block - 1] if block else wrap, downs[block])
-                weight = kept[level, :, pl.ds(block * LANES, LANES)].astype(F32)
-                velocity_ref[1, level, :, pl.ds(block * LANES, LANES)] = (
-                    scale * (right - left) * weight
-                )
-
-    @pl.when(step < ROWS // 8)
-    def _():
-        kept[...] = mask_ref[...]
+                weight = kept[(step + 1) % 2, level, :, pl.ds(block * LANES, LANES)]
+                place_block(velocity_ref, 1, level, block, scale * (right - left) * weight)
 
 
 def body(control, land_mask, row_class, decay_rate, balance):
     wide = BLOCKS * LANES
     params = functools.partial(pltpu.CompilerParams, vmem_limit_bytes=LIMIT)
 
-    def like(*shape, dtype=F32):
-        return jax.ShapeDtypeStruct(shape, dtype)
+    def like(*shape):
+        return jax.ShapeDtypeStruct(shape, F32)
 
     columns = jnp.transpose(control, (2, 1, 0))
 
@@ -590,8 +597,8 @@
         in_specs=[
             SMEM,
             SMEM,
-            pl.BlockSpec((SECTOR, BAND, LANES), lambda g: (0, g, 0)),
-            pl.BlockSpec((LEVELS, BAND, wide), lambda g: (0, g, 0)),
+            pl.BlockSpec((SECTOR, BAND, COMP), lambda g: (0, g, 0)),
+            pl.BlockSpec((LEVELS, BAND, SECTOR), lambda g: (0, g, 0)),
         ],
         out_specs=[
             pl.BlockSpec((BAND, EXTENT, LANES), lambda g: (g, 0, 0)),
@@ -603,13 +610,13 @@
             pl.BlockSpec((2, ROWS, LANES), fixed3),
         ],
         out_shape=[
-            like(ROWS, EXTENT, LANES, dtype=BF16),
-            like(ROWS, PADDED, LANES),
-            like(2, PADDED, LANES),
-            like(2, ROWS, LANES),
-            like(8, LANES),
-            like(2, EXTENT, LANES),
-            like(2, ROWS, LANES),
+            pltpu.VMEM((ROWS, EXTENT, LANES), BF16),
+            pltpu.VMEM((ROWS, PADDED, LANES), F32),
+            pltpu.VMEM((2, PADDED, LANES), F32),
+            pltpu.VMEM((2, ROWS, LANES), F32),
+            pltpu.VMEM((8, LANES), F32),
+            pltpu.VMEM((2, EXTENT, LANES), F32),
+            pltpu.VMEM((2, ROWS, LANES), F32),
         ],
         scratch_shapes=[
             pltpu.VMEM((BLOCKS, BAND * PITCH, LANES), F32),
@@ -658,12 +665,12 @@
         in_specs=[
             pl.BlockSpec((8, EXTENT, LANES), lambda g: (jnp.minimum(g, 7), 0, 0)),
             pl.BlockSpec((8, EXTENT, LANES), lambda g: (jnp.minimum(g, 7), 0, 0)),
-            pl.BlockSpec((LEVELS, 8, wide), lambda g: (0, jnp.minimum(g, 7), 0)),
+            pl.BlockSpec((LEVELS, 8, SECTOR), lambda g: (0, jnp.minimum(g, 7), 0)),
             *[VMEM] * 6,
         ],
         out_specs=[
-            pl.BlockSpec((SECTOR, 8, LANES), lambda g: (0, jnp.minimum(g, 7), 0)),
-            pl.BlockSpec((2, LEVELS, 8, wide), lambda g: (0, 0, jnp.maximum(g - 1, 0), 0)),
+            pl.BlockSpec((SECTOR, 8, COMP), lambda g: (0, jnp.minimum(g, 7), 0)),
+            pl.BlockSpec((2, LEVELS, 8, SECTOR), lambda g: (0, 0, jnp.maximum(g - 1, 0), 0)),
         ],
         out_shape=[like(SECTOR, ROWS, COMP), like(2, LEVELS, ROWS, SECTOR)],
         scratch_shapes=[
@@ -673,10 +680,10 @@
             pltpu.VMEM((EXTENT * 8, LANES), F32),
             pltpu.VMEM((BLOCKS, 8 * PRESSURE_PITCH, LANES), F32),
             pltpu.VMEM((BLOCKS, (ROWS + 2) * PRESSURE_PITCH, LANES), F32),
-            pltpu.VMEM((LEVELS, 8, wide), jnp.int32),
+            pltpu.VMEM((2, LEVELS, 8, wide), F32),
             pltpu.VMEM((ROWS, LANES), F32),
         ],
-        compiler_params=params(),
+        compiler_params=pltpu.CompilerParams(vmem_limit_bytes=24 * 1024 * 1024),
         name="final",
     )(s, weight, land_mask, inflow, response, below, rims, edges, balance)
     return jnp.transpose(increment, (2, 1, 0)), velocity

time: 66.3 us -> 60.9 us (0.919)
  Pallas kernels: 64.6 us -> 59.1 us
    pallas_call x1, Pallas kernels: 18.9 us -> 14.8 us  [body(): pl.pallas_call(final_kernel, grid=(ROWS // 8 + 1,), in_specs=[pl.BlockSpe...]
    pallas_call x1, Pallas kernels: 45.7 us -> 44.3 us  [body(): pl.pallas_call(analysis_kernel, grid=(BANDS,), in_specs=[SMEM, SMEM, pl.B...]
where the time goes in v4:
time: 60.9 us; the launch traced here: 59.8 us
  Pallas kernels  59.1 us (97%)
  between operations  0.67 us (1%)
    pallas_call x1, Pallas kernels, body(): pl.pallas_call(analysis_kernel, grid=(BANDS,), in_specs=[SMEM, SMEM, pl.B...  44.3 us
    pallas_call x1, Pallas kernels, body(): pl.pallas_call(final_kernel, grid=(ROWS // 8 + 1,), in_specs=[pl.BlockSpe...  14.8 us

profile of v4, /device:TPU:0, one launch (start us, length us, event | category | flops | bytes accessed | tf_op | source)
XLA Modules:
  0.0 59.8 jit_solution(14233813498124678482)
XLA Ops:
  0.6 0.0 copy-start
  0.6 0.0 copy-start.1
  0.7 44.3 %analysis.1 = (bf16[64,272,128]{2,1,0:T(8,128)(2,1)S(1)}, f32[64,280,128]{2,1,0:T(8,128)S(1)}, f32[2,280,128]{2,1,0:T(8,128)S(1)}, f32[2,64,128]{2,1,0:T(8,128)S...) custom-call(s32[64]{0:T(128)} %class_ref.1, f32[16]{0:T(128)} %rate_ref.1, ...), custom_call_target="tpu_custom_call" | custom-call | tf_op jit(solution)/shard_map/analysis/pallas_call | solution.py:594
  45.0 0.0 copy-done
  45.0 0.0 copy-done.1
  45.0 14.8 %final.1 = (f32[270,64,120]{2,1,0:T(8,128)}, f32[2,30,64,270]{3,2,1,0:T(8,128)}) custom-call(f32[64,280,128]{2,1,0:T(8,128)S(1)} %get-tuple-element.11.s_ref, bf16[64,272,128]{2,1,0:T(8,128)(2,1)S(1)} %get-tuple-element.12.weight_ref, s32[30,64,270]{2,1,0:T(8,128)S(1)} %copy-done, f32[2,280,128]{2,1,0:T(8,128)S(1)} %get-tuple-element.13.inflow_ref, ...), custom_call_target="tpu_custom_call" | custom-call | tf_op jit(solution)/shard_map/final/pallas_call | solution.py:662
Async XLA Ops:
  0.6 44.4 %copy-start = (s32[30,64,270]{2,1,0:T(8,128)S(1)}, s32[30,64,270]{2,1,0:T(8,128)}, u32[]{:S(2)}) copy-start(s32[30,64,270]{2,1,0:T(8,128)} %mask_ref.3) | copy-start | bytes 6220804
  0.6 44.4 %copy-start.1 = (f32[120,120]{1,0:T(8,128)S(1)}, f32[120,120]{1,0:T(8,128)}, u32[]{:S(2)}) copy-start(f32[120,120]{1,0:T(8,128)} %balance_ref.1) | copy-start | bytes 172804

commit v5 on v4

--- a/solution.py
+++ b/solution.py
@@ -136,18 +136,29 @@
     def part(index):
         return pl.ds(pl.multiple_of(index * SHARE, 8), SHARE)
 
-    def share_copy(index, slot):
+    def share_copy(side, index, slot):
         return remote(
-            closing.at[:, part(index)], lat_first.at[slot], share_send.at[index], share_sem.at[slot], (index, lon)
+            closing.at[side, part(index)], lat_first.at[slot, side],
+            share_send.at[side, index], share_sem.at[side, slot], (index, lon),
         )
 
-    def share_arrival(slot):
-        return remote(lat_first.at[slot], lat_first.at[slot], share_send.at[slot], share_sem.at[slot], (slot, lon))
-
-    def reply_copy(to, index):
+    def share_arrival(side, slot):
         return remote(
-            lat_second.at[to], inflow_in.at[:, part(index)], reply_send.at[to], reply_sem.at[index], (to, lon)
+            lat_first.at[slot, side], lat_first.at[slot, side],
+            share_send.at[side, slot], share_sem.at[side, slot], (slot, lon),
         )
+
+    def reply_copy(side, to, index):
+        return remote(
+            lat_second.at[to, side], inflow_in.at[side, part(index)],
+            reply_send.at[side, to], reply_sem.at[side, index], (to, lon),
+        )
+
+    def far_lat(k):
+        return lat_peer(lax.rem(k + 2, LAT - 1) + 1)
+
+    def far_lon(k):
+        return lon_peer(lax.rem(k + 6, LON - 1) + 1)
 
     def out_copy(index):
         return pltpu.make_async_copy(field.at[:, part(index)], s_ref.at[:, part(index)], out_sem.at[index])
@@ -302,7 +313,7 @@
     for half in range(BAND // 8):
         for side, value in enumerate((east, west)):
             ew[step, 2 * half + side] = value[half * 8 : half * 8 + 8]
-    each(LON, lambda k: closing_copy(step, lon_peer(k), lon).start())
+    each(LON, lambda k: closing_copy(step, far_lon(k), lon).start())
     gathered[step, lon] = ew[step]
 
     @pl.when(step == BANDS - 1)
@@ -375,10 +386,25 @@
     def _():
         lax.fori_loop(0, BANDS, forward_band, 0)
         closing[0] = state[...]
+
+        def send_north(k, c):
+            index = lax.rem(lat + 1 + k, SHARES)
+
+            @pl.when(index != lat)
+            def _():
+                share_copy(0, index, lat).start()
+
+            @pl.when(index == lat)
+            def _():
+                lat_first[lat, 0] = closing[0, part(lat)]
+
+            return c
+
+        lax.fori_loop(0, SHARES, send_north, 0)
         each(LAT, lambda k: rate_copy(lat_peer(k), lat_peer(k)).wait_recv())
 
         def strip(turn, _):
-            index = lax.rem(lat + turn, SHARES)
+            index = lax.rem(lat + 1 + turn, SHARES)
             base = pl.multiple_of(index * SHARE, 8)
 
             def one_row(k, south):
@@ -399,28 +425,33 @@
 
             @pl.when(index != lat)
             def _():
-                share_copy(index, lat).start()
+                share_copy(1, index, lat).start()
 
             @pl.when(index == lat)
             def _():
-                lat_first[lat] = closing[:, part(lat)]
+                lat_first[lat, 1] = closing[1, part(lat)]
+
+            @pl.when((lat < SHARES) & (turn == SHARES - 2))
+            def _():
+                each(LAT, lambda k: share_arrival(0, lat_peer(k)).wait_recv())
+                lat_second[0, 0] = jnp.zeros((SHARE, LANES), F32)
+                for t in range(LAT - 1):
+                    lat_second[t + 1, 0] = lat_first[t, 0] + others[t, 0:1, :] * lat_second[t, 0]
+                each(LAT, lambda k: reply_copy(0, far_lat(k), lat).start())
+                inflow_in[0, part(lat)] = lat_second[lat, 0]
 
             @pl.when((lat < SHARES) & (turn == SHARES - 1))
             def _():
-                each(LAT, lambda k: share_arrival(lat_peer(k)).wait_recv())
-                blank = jnp.zeros((SHARE, LANES), F32)
-                lat_second[0, 0] = blank
-                for t in range(LAT - 1):
-                    lat_second[t + 1, 0] = lat_first[t, 0] + others[t, 0:1, :] * lat_second[t, 0]
-                lat_second[LAT - 1, 1] = blank
+                each(LAT, lambda k: share_arrival(1, lat_peer(k)).wait_recv())
+                lat_second[LAT - 1, 1] = jnp.zeros((SHARE, LANES), F32)
                 for t in range(LAT - 1, 0, -1):
                     lat_second[t - 1, 1] = (
                         lat_first[t, 1]
                         + others[t, 1:2, :] * lat_second[t, 0]
                         + others[t, 0:1, :] * lat_second[t, 1]
                     )
-                each(LAT, lambda k: reply_copy(lat_peer(k), lat).start())
-                inflow_in[:, part(lat)] = lat_second[lat]
+                each(LAT, lambda k: reply_copy(1, far_lat(k), lat).start())
+                inflow_in[1, part(lat)] = lat_second[lat, 1]
 
             return 0
 
@@ -439,8 +470,9 @@
         def settle(index, c):
             @pl.when(index != lat)
             def _():
-                share_copy(index, lat).wait_send()
-                reply_copy(index, index).wait_recv()
+                for side in range(2):
+                    share_copy(side, index, lat).wait_send()
+                    reply_copy(side, index, index).wait_recv()
 
             out_copy(index).wait()
             return c
@@ -449,7 +481,8 @@
 
         @pl.when(lat < SHARES)
         def _():
-            each(LAT, lambda k: reply_copy(lat_peer(k), lat).wait_send())
+            for side in range(2):
+                each(LAT, lambda k: reply_copy(side, lat_peer(k), lat).wait_send())
 
         inflow_ref[...] = inflow_in[...]
 
@@ -649,10 +682,10 @@
             dma((2,)),
             dma((LAT,)),
             dma((LAT,)),
-            dma((LAT,)),
-            dma((LAT,)),
-            dma((LAT,)),
-            dma((LAT,)),
+            dma((2, LAT)),
+            dma((2, LAT)),
+            dma((2, LAT)),
+            dma((2, LAT)),
             dma((SHARES,)),
         ],
         compiler_params=params(collective_id=0, has_side_effects=True),

time: 60.9 us -> 60.1 us (0.987); the launches traced: 59.8 us -> 60 us
  no operation moved by 1% of the time
where the time goes in v5:
time: 60.1 us; the launch traced here: 60 us
  Pallas kernels  59.3 us (99%)
  between operations  0.67 us (1%)
    pallas_call x1, Pallas kernels, body(): pl.pallas_call(analysis_kernel, grid=(BANDS,), in_specs=[SMEM, SMEM, pl.B...  44.5 us
    pallas_call x1, Pallas kernels, body(): pl.pallas_call(final_kernel, grid=(ROWS // 8 + 1,), in_specs=[pl.BlockSpe...  14.8 us

profile of v5, /device:TPU:0, one launch (start us, length us, event | category | flops | bytes accessed | tf_op | source)
XLA Modules:
  0.0 60.0 jit_solution(12421691046002940331)
XLA Ops:
  0.6 0.0 copy-start
  0.6 0.0 copy-start.1
  0.7 44.5 %analysis.1 = (bf16[64,272,128]{2,1,0:T(8,128)(2,1)S(1)}, f32[64,280,128]{2,1,0:T(8,128)S(1)}, f32[2,280,128]{2,1,0:T(8,128)S(1)}, f32[2,64,128]{2,1,0:T(8,128)S...) custom-call(s32[64]{0:T(128)} %class_ref.1, f32[16]{0:T(128)} %rate_ref.1, ...), custom_call_target="tpu_custom_call" | custom-call | tf_op jit(solution)/shard_map/analysis/pallas_call | solution.py:627
  45.2 0.0 copy-done
  45.2 0.0 copy-done.1
  45.2 14.8 %final.1 = (f32[270,64,120]{2,1,0:T(8,128)}, f32[2,30,64,270]{3,2,1,0:T(8,128)}) custom-call(f32[64,280,128]{2,1,0:T(8,128)S(1)} %get-tuple-element.11.s_ref, bf16[64,272,128]{2,1,0:T(8,128)(2,1)S(1)} %get-tuple-element.12.weight_ref, s32[30,64,270]{2,1,0:T(8,128)S(1)} %copy-done, f32[2,280,128]{2,1,0:T(8,128)S(1)} %get-tuple-element.13.inflow_ref, ...), custom_call_target="tpu_custom_call" | custom-call | tf_op jit(solution)/shard_map/final/pallas_call | solution.py:695
Async XLA Ops:
  0.6 44.5 %copy-start = (s32[30,64,270]{2,1,0:T(8,128)S(1)}, s32[30,64,270]{2,1,0:T(8,128)}, u32[]{:S(2)}) copy-start(s32[30,64,270]{2,1,0:T(8,128)} %mask_ref.3) | copy-start | bytes 6220804
  0.6 44.5 %copy-start.1 = (f32[120,120]{1,0:T(8,128)S(1)}, f32[120,120]{1,0:T(8,128)}, u32[]{:S(2)}) copy-start(f32[120,120]{1,0:T(8,128)} %balance_ref.1) | copy-start | bytes 172804

commit v6 on v5

--- a/solution.py
+++ b/solution.py
@@ -291,12 +291,12 @@
     nothing = jnp.zeros((BAND, LANES), F32)
     pairs = SECTOR // 2
     carried = lax.fori_loop(
-        0, pairs // 2 - 1, lambda p, c: advance(p, c, False, False), (nothing, nothing), unroll=3
+        0, pairs // 2 - 1, lambda p, c: advance(p, c, False, False), (nothing, nothing), unroll=6
     )
     carried = advance(pairs // 2 - 1, carried, False, False)
     carried = advance(pairs // 2, carried, False, True)
     carried = lax.fori_loop(
-        pairs // 2 + 1, pairs - 1, lambda p, c: advance(p, c, True, True), carried, unroll=3
+        pairs // 2 + 1, pairs - 1, lambda p, c: advance(p, c, True, True), carried, unroll=6
     )
     east, west = advance(pairs - 1, carried, True, True)
     columns[spot(SECTOR)] = keep * east
@@ -584,7 +584,7 @@
             increment_ref[j] = mixed[pl.ds(pl.multiple_of(j * 8, 8), 8), :COMP]
             return 0
 
-        lax.fori_loop(0, SECTOR, place, 0, unroll=10)
+        lax.fori_loop(0, SECTOR, place, 0, unroll=27)
 
     @pl.when(step > 0)
     def _():

time: 60.1 us -> 59.5 us (0.990)
  no operation moved by 1% of the time
where the time goes in v6:
time: 59.5 us; the launch traced here: 59.4 us
  Pallas kernels  58.7 us (99%)
  between operations  0.67 us (1%)
    pallas_call x1, Pallas kernels, body(): pl.pallas_call(analysis_kernel, grid=(BANDS,), in_specs=[SMEM, SMEM, pl.B...  44.4 us
    pallas_call x1, Pallas kernels, body(): pl.pallas_call(final_kernel, grid=(ROWS // 8 + 1,), in_specs=[pl.BlockSpe...  14.3 us

profile of v6, /device:TPU:0, one launch (start us, length us, event | category | flops | bytes accessed | tf_op | source)
XLA Modules:
  0.0 59.4 jit_solution(5884341032253826095)
XLA Ops:
  0.6 0.0 copy-start
  0.6 0.0 copy-start.1
  0.7 44.4 %analysis.1 = (bf16[64,272,128]{2,1,0:T(8,128)(2,1)S(1)}, f32[64,280,128]{2,1,0:T(8,128)S(1)}, f32[2,280,128]{2,1,0:T(8,128)S(1)}, f32[2,64,128]{2,1,0:T(8,128)S...) custom-call(s32[64]{0:T(128)} %class_ref.1, f32[16]{0:T(128)} %rate_ref.1, ...), custom_call_target="tpu_custom_call" | custom-call | tf_op jit(solution)/shard_map/analysis/pallas_call | solution.py:627
  45.1 0.0 copy-done
  45.1 0.0 copy-done.1
  45.1 14.3 %final.1 = (f32[270,64,120]{2,1,0:T(8,128)}, f32[2,30,64,270]{3,2,1,0:T(8,128)}) custom-call(f32[64,280,128]{2,1,0:T(8,128)S(1)} %get-tuple-element.11.s_ref, bf16[64,272,128]{2,1,0:T(8,128)(2,1)S(1)} %get-tuple-element.12.weight_ref, s32[30,64,270]{2,1,0:T(8,128)S(1)} %copy-done, f32[2,280,128]{2,1,0:T(8,128)S(1)} %get-tuple-element.13.inflow_ref, ...), custom_call_target="tpu_custom_call" | custom-call | tf_op jit(solution)/shard_map/final/pallas_call | solution.py:695
Async XLA Ops:
  0.6 44.5 %copy-start = (s32[30,64,270]{2,1,0:T(8,128)S(1)}, s32[30,64,270]{2,1,0:T(8,128)}, u32[]{:S(2)}) copy-start(s32[30,64,270]{2,1,0:T(8,128)} %mask_ref.3) | copy-start | bytes 6220804
  0.6 44.5 %copy-start.1 = (f32[120,120]{1,0:T(8,128)S(1)}, f32[120,120]{1,0:T(8,128)}, u32[]{:S(2)}) copy-start(f32[120,120]{1,0:T(8,128)} %balance_ref.1) | copy-start | bytes 172804
